TPU v7x, 256 devices: a whole 4x4x8 slice. The times are simulated.
256 devices in a mesh: section: 4 (over z_lo, core), seq: 4 (over y), head: 16 (over x, z_hi).
Axes of the slice: x: 4, y: 4, z: 8 (z_hi: 4, z_lo: 2; z = z_hi * 2 + z_lo), core: 2. Of those that a mesh axis runs over, the one named last changes fastest.
Arguments:
- hidden: bfloat16 [4, 2048, 4608], P(None, ('section', 'seq'), 'head')
- critique: bfloat16 [4, 4, 4608], P('seq', None, 'head')
- lengths: int32 [4], replicated, may hold values from 512 to 2048, as said below
- pre_gain: bfloat16 [4608], replicated, may hold values from 0.099609375 to 1.8984375
- post_gain: bfloat16 [4608], P('head'), may hold values from 0.099609375 to 1.8984375
- q_weight: bfloat16 [4608, 4096], P(None, 'head'), may hold values from -0.09375 to 0.09375
- k_weight: bfloat16 [4608, 2048], P(None, 'head'), may hold values from -0.09375 to 0.09375
- v_weight: bfloat16 [4608, 2048], P(None, 'head')
- o_weight: bfloat16 [4096, 4608], P('head')
Outputs:
- hidden_out: bfloat16 [4, 2048, 4608], P(None, ('section', 'seq'), 'head')
- critique_out: bfloat16 [4, 4, 4608], P('seq', None, 'head')
Inputs may be any that keep to these rules, and one draw needn't show every extreme that they name: `lengths`: one pair fills all 2048 slots and one uses 2048/4 of them.
All inputs are finite; a program needn't handle non-finite values.
Results may differ from a plain program's by a relative error of at most 0.007.
Values may be sent and summed in bfloat16 or wider, within the bound.
A program may use at most 128 MiB of HBM per device.

v0:
```python
import math

import jax
import jax.numpy as jnp
from jax import lax
from jax.sharding import PartitionSpec as P

D = 4608
HEADS = 32
KV_HEADS = 16
HEAD = 128


epsilon = 1e-06
soft_cap = 50.0
rope_base = 10000.0


def norm_scale(inputs, gain_vector):
    floats = inputs.astype(jnp.float32)
    mean_square = jnp.mean(floats * floats, axis=-1, keepdims=True)
    return (floats * lax.rsqrt(mean_square + epsilon) * gain_vector.astype(jnp.float32)).astype(
        jnp.bfloat16
    )


def rotate(inputs, positions):
    half_size = inputs.shape[-1] // 2
    frequency = jnp.exp(
        jnp.arange(half_size, dtype=jnp.float32) * (-2.0 * math.log(rope_base) / inputs.shape[-1])
    )
    rotation = positions[..., None, None] * frequency
    cosine = jnp.cos(rotation)
    sine_part = jnp.sin(rotation)
    front_half = inputs[..., :half_size]
    second = inputs[..., half_size:]
    return jnp.concatenate(
        [front_half * cosine - second * sine_part, second * cosine + front_half * sine_part],
        axis=-1,
    )


def partial_sums(query_rows, key_rows, value_rows, key_mask, score_scale):
    scores = (
        jnp.einsum("rtgjd,rkgd->rtgjk", query_rows, key_rows, preferred_element_type=jnp.float32)
        * score_scale
    )
    scores = soft_cap * jnp.tanh(scores / soft_cap)
    weight = jnp.where(key_mask[:, :, None, None, :], jnp.exp(scores), 0.0)
    weight_total = jnp.sum(weight, axis=-1)
    summed = jnp.einsum(
        "rtgjk,rkgd->rtgjd",
        weight.astype(jnp.bfloat16),
        value_rows,
        preferred_element_type=jnp.float32,
    )
    return (summed, weight_total)


def body(hidden, critique, lengths, pre_gain, post_gain, q_weight, k_weight, v_weight, o_weight):
    row_count, local_span, local_width = hidden.shape
    step_count = critique.shape[1]
    group_size = HEADS // KV_HEADS
    q_width = q_weight.shape[1]
    kv_here = k_weight.shape[1] // HEAD
    score_scale = (D // HEADS) ** (-0.5)
    shard_place = lax.axis_index(("section", "seq"))
    token_index = shard_place * local_span + jnp.arange(local_span, dtype=jnp.int32)
    positions = jnp.broadcast_to(token_index.astype(jnp.float32)[None, :], (row_count, local_span))
    flat_count = row_count * local_span
    gathered = lax.all_gather(hidden, "head", axis=2, tiled=True)
    normed = norm_scale(gathered, pre_gain).reshape(flat_count, D)
    queries = jnp.dot(normed, q_weight, preferred_element_type=jnp.float32)
    key_rows = jnp.dot(normed, k_weight, preferred_element_type=jnp.float32)
    value_rows = jnp.dot(normed, v_weight, preferred_element_type=jnp.float32)
    value_rows = value_rows.astype(jnp.bfloat16).reshape(row_count, local_span, kv_here, HEAD)
    queries = rotate(queries.reshape(row_count, local_span, kv_here * group_size, HEAD), positions)
    queries = queries.astype(jnp.bfloat16).reshape(row_count, local_span, kv_here, group_size, HEAD)
    key_rows = rotate(key_rows.reshape(row_count, local_span, kv_here, HEAD), positions).astype(
        jnp.bfloat16
    )
    piece_keys = lax.all_gather(key_rows, ("section", "seq"), axis=1, tiled=True)
    piece_values = lax.all_gather(value_rows, ("section", "seq"), axis=1, tiled=True)
    key_index = jnp.arange(piece_keys.shape[1], dtype=jnp.int32)
    key_mask = (key_index[None, None, :] <= token_index[None, :, None]) & (
        key_index[None, None, :] < lengths[:, None, None]
    )
    summed, weight_total = partial_sums(queries, piece_keys, piece_values, key_mask, score_scale)
    summed, weight_total = (summed, weight_total)
    attended = (summed / weight_total[..., None]).astype(jnp.bfloat16).reshape(flat_count, q_width)
    projected = jnp.dot(attended, o_weight, preferred_element_type=jnp.float32)
    share = lax.psum_scatter(
        projected.astype(jnp.bfloat16), "head", scatter_dimension=1, tiled=True
    ).astype(jnp.float32)
    share_squares = lax.psum(jnp.sum(share * share, axis=-1), "head")
    flat_hidden = hidden.reshape(flat_count, local_width).astype(jnp.float32)
    hidden_out = flat_hidden + share * lax.rsqrt(share_squares / D + epsilon)[
        :, None
    ] * post_gain.astype(jnp.float32)
    hidden_out = hidden_out.astype(jnp.bfloat16).reshape(row_count, local_span, local_width)
    critique_rows = critique.shape[0]
    features = lax.all_gather(critique, "head", axis=2, tiled=True)
    cache_keys, cache_values = (
        lax.all_to_all(key_rows, "seq", split_axis=0, concat_axis=1, tiled=True),
        lax.all_to_all(value_rows, "seq", split_axis=0, concat_axis=1, tiled=True),
    )
    row_lengths = lax.dynamic_slice_in_dim(
        lengths, lax.axis_index("seq") * critique_rows, critique_rows
    )
    batch_rows = features.shape[0]
    normed = norm_scale(features, pre_gain).reshape(batch_rows * step_count, D)
    step_positions = (
        row_lengths[:, None] + jnp.arange(step_count, dtype=jnp.int32)[None, :]
    ).astype(jnp.float32)
    new_queries = jnp.dot(normed, q_weight, preferred_element_type=jnp.float32).reshape(
        batch_rows, step_count, kv_here * group_size, HEAD
    )
    new_queries = (
        rotate(new_queries, step_positions)
        .astype(jnp.bfloat16)
        .reshape(batch_rows, step_count, kv_here, group_size, HEAD)
    )
    new_keys = jnp.dot(normed, k_weight, preferred_element_type=jnp.float32).reshape(
        batch_rows, step_count, kv_here, HEAD
    )
    new_keys = rotate(new_keys, step_positions).astype(jnp.bfloat16)
    new_values = jnp.dot(normed, v_weight, preferred_element_type=jnp.float32).astype(jnp.bfloat16)
    new_queries, new_keys, new_values = (
        new_queries,
        new_keys,
        new_values.reshape(batch_rows, step_count, kv_here, HEAD),
    )
    key_start = lax.axis_index("section") * cache_keys.shape[1]
    key_index = key_start + jnp.arange(cache_keys.shape[1], dtype=jnp.int32)
    key_mask = jnp.broadcast_to(
        key_index[None, None, :] < row_lengths[:, None, None],
        (new_queries.shape[0], step_count, cache_keys.shape[1]),
    )
    far_sum, far_total = partial_sums(new_queries, cache_keys, cache_values, key_mask, score_scale)
    far_sum, far_total = lax.psum((far_sum, far_total), "section")
    step_order = jnp.arange(step_count, dtype=jnp.int32)
    key_mask = (step_order[None, :] <= step_order[:, None])[None]
    near_sum, near_total = partial_sums(new_queries, new_keys, new_values, key_mask, score_scale)
    new_attended = ((far_sum + near_sum) / (far_total + near_total)[..., None]).astype(jnp.bfloat16)
    new_projected = jnp.dot(
        new_attended.reshape(critique_rows * step_count, q_width),
        o_weight,
        preferred_element_type=jnp.float32,
    )
    new_share = lax.psum_scatter(
        new_projected.astype(jnp.bfloat16), "head", scatter_dimension=1, tiled=True
    ).astype(jnp.float32)
    new_squares = lax.psum(jnp.sum(new_share * new_share, axis=-1), "head")
    flat_critique = critique.reshape(critique_rows * step_count, local_width).astype(jnp.float32)
    critique_out = flat_critique + new_share * lax.rsqrt(new_squares / D + epsilon)[
        :, None
    ] * post_gain.astype(jnp.float32)
    critique_out = critique_out.astype(jnp.bfloat16).reshape(critique_rows, step_count, local_width)
    return (hidden_out, critique_out)


def solution(mesh):
    return jax.shard_map(
        body,
        mesh=mesh,
        in_specs=(
            P(None, ("section", "seq"), "head"),
            P("seq", None, "head"),
            P(),
            P(),
            P("head"),
            P(None, "head"),
            P(None, "head"),
            P(None, "head"),
            P("head", None),
        ),
        out_specs=(P(None, ("section", "seq"), "head"), P("seq", None, "head")),
        check_vma=False,
    )
```

profile of v0, /device:TPU:32, one launch (start us, length us, event | category | flops | bytes accessed | tf_op | source)
XLA Modules:
  0.0 507.2 jit_solution(6736168550141121859)
XLA Ops:
  7.2 2.0 copy.77
  9.3 1.3 convert_element_type.111
  11.1 84.3 %all-gather.4.cloned.1.call-done = bf16[4,128,4608]{1,0,2:T(4,128)(2,1)} async-done(((bf16[4,128,288]{1,0,2:T(4,128)(2,1)}), bf16[4,128,4608]{1,0,2:T(4,128)(2,1)}) %all-gather.4.cloned.1.call-update) | async-done | bytes 4718608 | tf_op jit(solution)/shard_map/all_gather | solution.py:71
  95.4 8.4 %copy.78 = bf16[4,128,4608]{2,1,0:T(8,128)(2,1)} copy(bf16[4,128,4608]{1,0,2:T(4,128)(2,1)} %all-gather.4.cloned.1.call-done) | data formatting | bytes 9437184 | tf_op jit(solution)/shard_map/all_gather | solution.py:71
  103.8 3.5 fusion
  107.6 2.3 fusion.2
  109.9 2.1 copy-done.2
  112.1 1.7 fusion.21
  115.7 77.7 %all_gather.15 = bf16[1,4,4608]{1,0,2:T(2,128)(2,1)} all-gather(bf16[1,4,288]{1,0,2:T(2,128)(2,1)} %copy.89), channel_id=1, replica_groups=mesh['section'=4,'seq'=4,'head'=16] {'head'}, dimensions={2}, use_global_device_ids=true | all-gather | bytes 39168 | tf_op jit(solution)/shard_map/all_gather | solution.py:102
  193.4 5.7 %copy.90 = bf16[1,4,4608]{2,1,0:T(4,128)(2,1)} copy(bf16[1,4,4608]{1,0,2:T(2,128)(2,1)} %all_gather.15) | data formatting | bytes 73728 | tf_op jit(solution)/shard_map/all_gather | solution.py:102
  202.9 1.6 fusion.38
  204.8 4.7 convolution_convert_fusion.2
  209.5 1.7 copy.79
  211.2 1.2 add_compare_fusion
  212.5 4.3 copy.108
  216.8 2.4 convolution_bitcast_fusion.2
  221.2 1.6 broadcast_and_fusion
  222.8 6.6 %all-to-all-start.1 = ((bf16[4,128,1,128]{1,3,2,0:T(8,128)(2,1)}), bf16[4,128,1,128]{1,3,2,0:T(8,128)(2,1)S(1)}, u32[]{:S(2)}, u32[]{:S(2)}) async-start(bf16[4,128,1,128]{1,3,2,0:T(8,128)(2,1)} %get-tuple-element.20), calls=%async_computation.2 | async-start | bytes 262144 | tf_op jit(solution)/shard_map/all_to_all | solution.py:104
  229.5 4.2 fusion.5
  234.4 1.5 all-to-all-done.1
  236.0 3.9 all-to-all-start
  240.7 1.2 fusion.116
  241.9 4.0 all-to-all-done
  247.0 6.2 %all-reduce.1 = (f32[1,4,1,2,128]{4,1,3,2,0:T(4,128)S(1)}, f32[1,4,1,2]{1,3,2,0:T(2,128)S(1)}) all-reduce(f32[1,4,1,2,128]{4,1,3,2,0:T(4,128)S(1)} %convolution_bitcast_fusion, f32[1,4,1,2]{1,3,2,0:T(2,128)S(1)} %bitcast.216), channel_id=1, replica_groups=mesh['section'=4,'seq'=4,'head'=16] {'section'}, use_global_device_ids=true, to_apply=%region_6.7 | all-reduce | flops 1032 | bytes 8256 | tf_op jit(solution)/shard_map/psum | solution.py:140
  254.4 1.5 copy.106
  256.2 7.5 %fusion.3 = (f32[4,128,2]{1,2,0:T(2,128)S(1)}, f32[4,2048,128,2]{2,1,3,0:T(8,128)}) fusion(pred[4,128,2048]{1,2,0:T(8,128)(4,1)S(1)} %broadcast_and_fusion, bf16[4,128,2,64]{1,3,2,0:T(8,128)(2,1)} %get-tuple-element.17, bf16[4,128,2,64]{1,3,2,0:T(8,128)(2,1)} %get-tuple-element.16, bf16[4,2048,1,128]{1,3,0,2:T(8,128)(2,1)} %all-gather.8.cloned.1.call-done), kind=kOutput, calls=%fused_computation.7 | convolution fusion | flops 545782784 | bytes 11800576 | tf_op jit(solution)/shard_map/rtgjd,rkgd->rtgjk/dot_general | solution.py:45
  264.0 7.3 %fusion.50 = bf16[4,128,1,2,128]{1,4,3,0,2:T(8,128)(2,1)} fusion(f32[4,2048,128,2]{2,1,3,0:T(8,128)} %get-tuple-element.31, pred[4,128,2048]{1,2,0:T(8,128)(4,1)S(1)} %broadcast_and_fusion, bf16[4,2048,1,128]{1,3,0,2:T(8,128)(2,1)} %all-gather.6.cloned.1.call-done, f32[4,128,2]{1,2,0:T(2,128)S(1)} %get-tuple-element.30), kind=kOutput, calls=%fused_computation.50 | convolution fusion | flops 545521664 | bytes 11800576 | tf_op jit(solution)/shard_map/rtgjk,rkgd->rtgjd/dot_general | solution.py:51
  272.4 3.6 convolution_convert_fusion
  276.0 77.6 %reduce-scatter.7.cloned.1.call-done = bf16[288,4]{1,0:T(8,128)(2,1)} async-done(((bf16[4608,4]{1,0:T(8,128)(2,1)}), bf16[288,4]{1,0:T(8,128)(2,1)}) %reduce-scatter.7.cloned.1.call-update) | async-done | bytes 2320
  354.7 99.2 %reduce-scatter.5.cloned.1.call-done = bf16[512,288]{0,1:T(8,128)(2,1)} async-done(((bf16[512,4608]{0,1:T(8,128)(2,1)}), bf16[512,288]{0,1:T(8,128)(2,1)}) %reduce-scatter.5.cloned.1.call-update) | async-done | bytes 294928 | tf_op jit(solution)/shard_map/reduce_scatter | solution.py:92
  454.9 43.2 %all-reduce = (f32[512]{0:T(512)S(1)}, f32[4]{0:T(128)S(1)}) all-reduce(f32[512]{0:T(512)S(1)} %fusion.55, f32[4]{0:T(128)S(1)} %fusion.81), channel_id=1, replica_groups=mesh['section'=4,'seq'=4,'head'=16] {'head'}, use_global_device_ids=true, to_apply=%region_4.5 | all-reduce | flops 516 | bytes 4128 | tf_op jit(solution)/shard_map/psum | solution.py:95
  498.9 1.8 copy_bitcast_fusion
  (83 shorter events, 17.2 us)
Async XLA Ops:
  7.2 246.6 %copy-start = (bf16[256,4608]{1,0:T(8,128)(2,1)S(1)}, bf16[256,4608]{1,0:T(8,128)(2,1)}, u32[]{:S(2)}) copy-start(bf16[256,4608]{1,0:T(8,128)(2,1)} %param.17) | copy-start | bytes 7077892
  7.2 88.2 %all-gather.4.cloned.1.call-start = ((), (), s32[]{:S(2)}) async-start(), calls=%async_computation.4 | async-start | bytes 5013504 | tf_op jit(solution)/shard_map/all_gather | solution.py:71
  9.2 247.0 %all-gather.8.cloned.1.call-start = ((), (), s32[]{:S(2)}) async-start(), calls=%async_computation.6 | async-start | bytes 2228224 | tf_op jit(solution)/shard_map/all_gather | solution.py:82
  11.1 102.6 %copy-start.10 = (f32[128]{0:T(128)}, f32[128]{0:T(128)S(1)}, u32[]{:S(2)}) copy-start(f32[128]{0:T(128)S(1)} %get-tuple-element.37) | copy-start | bytes 1540
  103.8 3.8 copy-start.1
  107.6 4.5 copy-start.3
  109.9 2.1 copy-start.2
  112.1 2.7 copy-start.9
  112.1 87.0 %copy-start.17 = (s32[4]{0:T(128)S(1)}, s32[4]{0:T(128)}, u32[]{:S(2)}) copy-start(s32[4]{0:T(128)} %param.11) | copy-start | bytes 52
  114.8 149.2 %all-gather.6.cloned.1.call-start = ((), (), s32[]{:S(2)}) async-start(), calls=%async_computation.5 | async-start | bytes 2228224 | tf_op jit(solution)/shard_map/all_gather | solution.py:83
  204.8 12.0 %copy-start.5 = (bf16[1,4,4608]{2,1,0:T(4,128)(2,1)S(1)}, bf16[1,4,4608]{2,1,0:T(4,128)(2,1)}, u32[]{:S(2)}) copy-start(bf16[1,4,4608]{2,1,0:T(4,128)(2,1)} %copy.90) | copy-start | bytes 110596
  204.8 12.0 %copy-start.8 = (f32[4608]{0:T(1024)S(1)}, f32[4608]{0:T(1024)}, u32[]{:S(2)}) copy-start(f32[4608]{0:T(1024)} %convert_element_type.111) | copy-start | bytes 55300
  209.5 9.7 %copy-start.19 = (pred[4,4]{0,1:T(4,128)(4,1)S(1)}, pred[4,4]{0,1:T(4,128)(4,1)}, u32[]{:S(2)}) copy-start(pred[4,4]{0,1:T(4,128)(4,1)} %iota_compare_fusion.2) | copy-start | bytes 52
  209.5 10.5 %copy-start.11 = (f32[128]{0:T(128)S(1)}, f32[128]{0:T(128)}, u32[]{:S(2)}) copy-start(f32[128]{0:T(128)} %copy-done.10) | copy-start | bytes 1540
  209.5 11.4 %copy-start.18 = (s32[4]{0:T(128)S(1)}, s32[4]{0:T(128)}, u32[]{:S(2)}) copy-start(s32[4]{0:T(128)} %param.11) | copy-start | bytes 52
  209.5 11.5 %copy-start.16 = (s32[128]{0:T(128)S(1)}, s32[128]{0:T(128)}, u32[]{:S(2)}) copy-start(s32[128]{0:T(128)} %get-tuple-element.36) | copy-start | bytes 1540
  219.2 1.8 copy-start.12
  219.2 1.8 copy-start.14
  222.8 13.1 %all-to-all-start.1 = ((bf16[4,128,1,128]{1,3,2,0:T(8,128)(2,1)}), bf16[4,128,1,128]{1,3,2,0:T(8,128)(2,1)S(1)}, u32[]{:S(2)}, u32[]{:S(2)}) async-start(bf16[4,128,1,128]{1,3,2,0:T(8,128)(2,1)} %get-tuple-element.20), calls=%async_computation.2 | async-start | bytes 262144 | tf_op jit(solution)/shard_map/all_to_all | solution.py:104
  229.5 4.2 copy-start.6
  229.5 4.2 copy-start.7
  229.5 11.3 %copy-start.13 = (bf16[4,2,64]{2,0,1:T(4,128)(2,1)S(1)}, bf16[4,2,64]{2,0,1:T(4,128)(2,1)}, u32[]{:S(2)}) copy-start(bf16[4,2,64]{2,0,1:T(4,128)(2,1)} %copy-done.12) | copy-start | bytes 3076
  236.0 10.0 %all-to-all-start = ((bf16[4,128,1,128]{3,1,2,0:T(8,128)(2,1)}), bf16[4,128,1,128]{3,1,2,0:T(8,128)(2,1)}, u32[]{:S(2)}, u32[]{:S(2)}) async-start(bf16[4,128,1,128]{3,1,2,0:T(8,128)(2,1)} %bitcast.19), calls=%async_computation.1 | async-start | bytes 262144 | tf_op jit(solution)/shard_map/all_to_all | solution.py:105
  239.9 113.7 %reduce-scatter.7.cloned.1.call-start = ((), (), s32[]{:S(2)}) async-start(), calls=%async_computation.8 | async-start | bytes 1253376
  255.9 197.9 %reduce-scatter.5.cloned.1.call-start = ((), (), s32[]{:S(2)}) async-start(), calls=%async_computation.7 | async-start | bytes 5013504 | tf_op jit(solution)/shard_map/reduce_scatter | solution.py:92
  272.4 3.6 copy-start.15
  272.4 226.5 %copy-start.4 = (bf16[4,128,288]{1,2,0:T(8,128)(2,1)S(1)}, bf16[4,128,288]{1,2,0:T(8,128)(2,1)}, u32[]{:S(2)}) copy-start(bf16[4,128,288]{1,2,0:T(8,128)(2,1)} %param.9) | copy-start | bytes 884740
Sparse Core Ops, SparseCore 0:
  11.1 84.3 all-gather.3
  114.9 65.7 all-gather.7
  211.4 52.5 all-gather.5
  267.3 86.2 reduce-scatter.6
  357.1 96.7 reduce-scatter.4
where the time goes:
time: 510 us; the launch traced here: 507 us
  waiting for transfers between devices  267 us (52%)
  blocking collectives  127 us (25%)
  matrix products  37.6 us (7%)
  local copies, waits for them, and re-layouts  30.4 us (6%)
  other arithmetic  20.1 us (4%)
  between operations  14.1 us (3%)
  starting transfers between devices  10.9 us (2%)
    reduce_scatter x1, waiting for transfers between devices, body(): lax.psum_scatter(projected.astype(jnp.bfloat16), 'head', scatter_dimensio...  99.2 us
    all_gather x1, waiting for transfers between devices, body(): gathered = lax.all_gather(hidden, 'head', axis=2, tiled=True)  84.3 us
    all_gather x1, blocking collectives, body(): features = lax.all_gather(critique, 'head', axis=2, tiled=True)  77.7 us
    unnamed x6, waiting for transfers between devices  77.7 us
    psum x1, blocking collectives, body(): share_squares = lax.psum(jnp.sum(share * share, axis=-1), 'head')  43.2 us
  transfers between devices with their start and end apart: 7, of which 6 were waited for; matrix products, arithmetic and copies ran while one was open for 12% of the time, Pallas kernels for 0%

commit v1 on v0

v1 whole, which is shorter than its diff:
```python
import math

import jax
import jax.numpy as jnp
import numpy as np
from jax import lax
from jax.experimental import pallas as pl
from jax.experimental.pallas import tpu as pltpu
from jax.sharding import PartitionSpec as P

D = 4608
HEADS = 32
KV_HEADS = 16
HEAD = 128
ROWS = 4
SPAN = 128
WIDTH = 288
SLAB = 4 * WIDTH
HALF = WIDTH // 2
STEPS = 4

EPS = 1e-06
CAP = 50.0
BASE = 10000.0
SCALE = (D // HEADS) ** (-0.5)
F32 = jnp.float32
BF16 = jnp.bfloat16
MESH = pl.DeviceIdType.MESH
N_SEM = 160


def rope_table():
    freq = np.exp(np.arange(64, dtype=np.float64) * (-2.0 * math.log(BASE) / HEAD))
    angle = np.arange(2056, dtype=np.float64)[:, None] * freq
    return np.concatenate([np.cos(angle), np.sin(angle)], axis=-1).astype(np.float32)


def dot(a, b):
    return jnp.dot(a, b, preferred_element_type=F32)


def dot_t(a, b):
    return lax.dot_general(a, b, (((1,), (1,)), ((), ())), preferred_element_type=F32)


def kernel(
    hidden, critique, lengths, gains, table_hbm, wq, wk, wv, wo,
    out, c_out,
    xg, wraw, wt, gainb, pgb, xn, table, cosT, sinT, qbuf, kvg, attg, owslab, owt,
    pb, own, rs1, rs2, cg, cq, ckv, cattg, cpj, cown, crs, ssx, ssz,
    send_sem, recv_sem, local_sem,
):
    s = lax.axis_index("section")
    y = lax.axis_index("seq")
    h = lax.axis_index("head")
    x, z = h // 4, h % 4
    zlo, core = s // 2, s % 2

    def at_x(d):
        return {"head": ((x + d) % 4) * 4 + z}

    def at_z(d):
        return {"head": x * 4 + (z + d) % 4}

    def at_y(d):
        return {"seq": (y + d) % 4}

    to_zlo = {"section": (1 - zlo) * 2 + core}
    to_core = {"section": zlo * 2 + 1 - core}

    copies = {}

    def send(name, src, dst, device):
        i = len(copies)
        assert i < N_SEM
        copy = pltpu.make_async_remote_copy(
            src_ref=src, dst_ref=dst, send_sem=send_sem.at[i], recv_sem=recv_sem.at[i],
            device_id=device, device_id_type=MESH,
        )
        copy.start()
        copies[name] = copy

    def recv(name):
        copies[name].wait_recv()

    local = []

    def fetch(src, dst):
        copy = pltpu.make_async_copy(src, dst, local_sem.at[len(local)])
        copy.start()
        local.append(copy)
        return copy

    piece = pl.multiple_of(core * 128 + y * 32, 32)
    own_cols = pl.ds(pl.multiple_of(x * SLAB, 128), SLAB)
    fetch_w = [
        fetch(wq, wraw.at[:, 0:256]),
        fetch(wk, wraw.at[:, 256:384]),
        fetch(wv, wraw.at[:, 384:512]),
    ]
    fetch_table = fetch(table_hbm, table)
    fetch_o = fetch(wo.at[pl.ds(piece, 32), own_cols], owslab.at[0, pl.ds(piece, 32), :])

    def turn(value):
        return jnp.concatenate(
            [value[:, 0:128].T, value[:, 128:256].T, value[:, 256:288].T], axis=0
        )

    for r in range(ROWS):
        xg[r, 0, 0] = turn(hidden[r].astype(F32)).astype(BF16)
    c_rows = jnp.concatenate([critique[0].astype(F32), jnp.zeros((4, WIDTH), F32)], axis=0)
    c_pad = jnp.concatenate([c_rows[:, 256:288], jnp.zeros((8, 96), F32)], axis=1)
    cg[0, 0] = jnp.concatenate(
        [c_rows[:, 0:128], c_rows[:, 128:256], c_pad, jnp.zeros((8, 128), F32)], axis=0
    ).astype(BF16)

    ssx[0] = jnp.zeros((24, 128), F32)
    partners = [at_x(1), at_x(3), at_x(2), at_z(1), at_z(3), at_z(2), at_y(1), at_y(3), to_zlo, to_core]
    barrier = pltpu.get_barrier_semaphore()
    for partner in partners:
        pl.semaphore_signal(barrier, inc=1, device_id=partner, device_id_type=MESH)
    pl.semaphore_wait(barrier, len(partners))

    def z1(r):
        send(("z1", r, 0), xg.at[r, 0, 0], xg.at[r, 0, 3], at_z(1))
        send(("z1", r, 1), xg.at[r, 0, 0], xg.at[r, 0, 1], at_z(3))

    def x1a(r):
        send(("x1a", r, 0), xg.at[r, 0, 0], xg.at[r, 3, 0], at_x(1))
        send(("x1a", r, 1), xg.at[r, 0, 0], xg.at[r, 1, 0], at_x(3))

    def e1(r):
        recv(("z1", r, 0))
        send(("z2", r, 0), xg.at[r, 0, 3, 0:HALF], xg.at[r, 0, 2, 0:HALF], at_z(1))
        recv(("z1", r, 1))
        send(("z2", r, 1), xg.at[r, 0, 1, HALF:WIDTH], xg.at[r, 0, 2, HALF:WIDTH], at_z(3))

    def e2(r):
        recv(("z2", r, 0))
        recv(("z2", r, 1))
        send(("x1b", r, 0), xg.at[r, 0, 1:4], xg.at[r, 3, 1:4], at_x(1))
        send(("x1b", r, 1), xg.at[r, 0, 1:4], xg.at[r, 1, 1:4], at_x(3))

    def e3(r):
        recv(("x1a", r, 0))
        recv(("x1b", r, 0))
        send(("x2", r, 0), xg.at[r, 3, :, 0:HALF], xg.at[r, 2, :, 0:HALF], at_x(1))
        recv(("x1a", r, 1))
        recv(("x1b", r, 1))
        send(("x2", r, 1), xg.at[r, 1, :, HALF:WIDTH], xg.at[r, 2, :, HALF:WIDTH], at_x(3))

    def e4(r):
        recv(("x2", r, 0))
        recv(("x2", r, 1))

    def ow_x():
        for d in (1, 3, 2):
            cols = pl.ds(pl.multiple_of(((x + d) % 4) * SLAB, 128), SLAB)
            send(("ow", d), wo.at[pl.ds(piece, 32), cols], owslab.at[4 - d, pl.ds(piece, 32), :], at_x(d))

    def ow_y1():
        fetch_o.wait()
        for d in (1, 3, 2):
            recv(("ow", d))
        here = owslab.at[:, pl.ds(piece, 32), :]
        send("owy1r", here, here, at_y(1))
        send("owy1l", here, here, at_y(3))

    def ow_y2():
        low = pl.ds(pl.multiple_of(core * 128 + ((y + 3) % 4) * 32, 32), 16)
        high = pl.ds(pl.multiple_of(core * 128 + ((y + 1) % 4) * 32 + 16, 16), 16)
        recv("owy1r")
        send("owy2r", owslab.at[:, low, :], owslab.at[:, low, :], at_y(1))
        recv("owy1l")
        send("owy2l", owslab.at[:, high, :], owslab.at[:, high, :], at_y(3))

    def ow_core():
        recv("owy2r")
        recv("owy2l")
        half = owslab.at[:, pl.ds(pl.multiple_of(core * 128, 128), 128), :]
        send("owc", half, half, to_core)

    def ow_turn():
        recv("owc")

        def step(d, carry):
            turned = owslab[d].T
            for zz in range(4):
                row = pl.multiple_of(((zz - z + 4) % 4) * WIDTH, 32)
                owt[d, pl.ds(row, WIDTH), :] = turned[zz * WIDTH : (zz + 1) * WIDTH]
            return carry

        lax.fori_loop(0, 4, step, 0)

    def gain_tables():
        turned = gains[...].T
        for hh in range(16):
            for k in range(3):
                n = 128 if k < 2 else 32
                column = turned[0:n, hh * 3 + k : hh * 3 + k + 1]
                gainb[hh * WIDTH + k * 128 : hh * WIDTH + k * 128 + n, :] = jnp.broadcast_to(column, (n, 128))
        for k in range(3):
            n = 128 if k < 2 else 32
            pgb[k * 128 : k * 128 + n, :] = jnp.broadcast_to(turned[0:n, 48 + k : 49 + k], (n, 128))

    def rope_tables():
        fetch_table.wait()
        place = pl.multiple_of((s * 4 + y) * SPAN, SPAN)
        turned = table[pl.ds(place, SPAN), :].T
        cosT[...] = turned[0:64]
        sinT[...] = turned[64:128]

    def turn_weights(lo, hi):
        def step(c, carry):
            row = pl.multiple_of(c * 256, 256)
            wt[:, pl.ds(row, 256)] = wraw[pl.ds(row, 256), :].T
            return carry

        lax.fori_loop(lo, hi, step, 0)

    def source_head(b):
        return ((x + b // 4) % 4) * 4 + (z + b % 4) % 4

    def project(r):
        def squares(b, total):
            block = xg[r, b // 4, b % 4].astype(F32)
            return total + jnp.sum((block * block).reshape(WIDTH // 8, 8, 128), axis=0)

        total = lax.fori_loop(0, 16, squares, jnp.zeros((8, 128), F32))
        factor = lax.rsqrt(jnp.sum(total, axis=0, keepdims=True) / D + EPS)

        def scale(b, carry):
            rows = pl.ds(pl.multiple_of(source_head(b) * WIDTH, 32), WIDTH)
            block = xg[r, b // 4, b % 4].astype(F32)
            xn[rows, :] = (block * factor * gainb[rows, :]).astype(BF16)
            return carry

        lax.fori_loop(0, 16, scale, 0)
        qkv = dot(wt[...], xn[...])
        cosine, sine = cosT[...], sinT[...]

        def rotated(value):
            a, b = value[0:64], value[64:128]
            return jnp.concatenate([a * cosine - b * sine, b * cosine + a * sine], axis=0)

        qbuf[r, 0:128, :] = rotated(qkv[0:128]).T.astype(BF16)
        qbuf[r, 128:256, :] = rotated(qkv[128:256]).T.astype(BF16)
        kvg[r, 0, 0, 0, 0:128, :] = rotated(qkv[256:384]).astype(BF16)
        kvg[r, 0, 0, 0, 128:256, :] = qkv[384:512].astype(BF16)

    def kv1(r):
        send(("kv1", r), kvg.at[r, 0, 0, 0], kvg.at[r, 0, 0, 1], to_zlo)

    def kv2(r):
        recv(("kv1", r))
        send(("kv2", r, 0), kvg.at[r, 0, 0], kvg.at[r, 0, 3], at_y(1))
        send(("kv2", r, 1), kvg.at[r, 0, 0], kvg.at[r, 0, 1], at_y(3))

    def kv3(r):
        recv(("kv2", r, 0))
        send(("kv3", r, 0), kvg.at[r, 0, 3, 0], kvg.at[r, 0, 2, 0], at_y(1))
        recv(("kv2", r, 1))
        send(("kv3", r, 1), kvg.at[r, 0, 1, 1], kvg.at[r, 0, 2, 1], at_y(3))

    def kv4(r):
        recv(("kv3", r, 0))
        recv(("kv3", r, 1))
        send(("kv4", r), kvg.at[r, 0], kvg.at[r, 1], to_core)

    def key_start(b):
        dc, dy, dz = b // 8, (b // 2) % 4, b % 2
        section = ((zlo + dz) % 2) * 2 + (core + dc) % 2
        return (section * 4 + (y + dy) % 4) * SPAN

    def weigh(scores, keep):
        capped = CAP * jnp.tanh(scores * (SCALE / CAP))
        return jnp.where(keep, jnp.exp(capped), 0.0)

    def attend(r):
        recv(("kv4", r))
        queries = qbuf[r]
        length = lengths[r]
        first = (s * 4 + y) * SPAN
        token = first + lax.broadcasted_iota(jnp.int32, (256, 128), 0) % SPAN
        limit = jnp.minimum(token, length - 1)
        lane = lax.broadcasted_iota(jnp.int32, (256, 128), 1)

        def step(b, carry):
            num, den = carry
            keys = kvg.at[r, b // 8, (b // 2) % 4, b % 2]
            weight = weigh(dot(queries, keys[0:128, :]), lane + key_start(b) <= limit)
            return num + dot_t(weight.astype(BF16), keys[128:256, :]), den + weight

        zero = jnp.zeros((256, 128), F32)
        num, den = lax.fori_loop(0, 16, step, (zero, zero))
        result = num / jnp.sum(den, axis=-1, keepdims=True)
        attg[r, 0, :, 0:128] = result[0:128].astype(BF16)
        attg[r, 0, :, 128:256] = result[128:256].astype(BF16)

    def ax1(r):
        send(("ax1", r, 0), attg.at[r, 0], attg.at[r, 3], at_x(1))
        send(("ax1", r, 1), attg.at[r, 0], attg.at[r, 1], at_x(3))

    def ax2(r):
        recv(("ax1", r, 0))
        send(("ax2", r, 0), attg.at[r, 3, 0:64], attg.at[r, 2, 0:64], at_x(1))
        recv(("ax1", r, 1))
        send(("ax2", r, 1), attg.at[r, 1, 64:128], attg.at[r, 2, 64:128], at_x(3))

    def proj(r):
        recv(("ax2", r, 0))
        recv(("ax2", r, 1))
        for dz in (2, 1, 3, 0):
            rows = pl.ds(dz * WIDTH, WIDTH)
            part = dot_t(owt[0, rows, :], attg[r, 0])
            for d in range(1, 4):
                part = part + dot_t(owt[d, rows, :], attg[r, d])
            if dz:
                pb[r, dz] = part.astype(BF16)
            else:
                own[r] = part
            if dz == 2:
                send(("rs1", r, 0), pb.at[r, 2, 0:HALF], rs1.at[r, 0], at_z(1))
                send(("rs1", r, 1), pb.at[r, 2, HALF:WIDTH], rs1.at[r, 1], at_z(3))

    def rs_2(r):
        recv(("rs1", r, 0))
        pb[r, 1, 0:HALF] = (pb[r, 1, 0:HALF].astype(F32) + rs1[r, 0].astype(F32)).astype(BF16)
        send(("rs2", r, 0), pb.at[r, 1], rs2.at[r, 0], at_z(1))
        recv(("rs1", r, 1))
        pb[r, 3, HALF:WIDTH] = (pb[r, 3, HALF:WIDTH].astype(F32) + rs1[r, 1].astype(F32)).astype(BF16)
        send(("rs2", r, 1), pb.at[r, 3], rs2.at[r, 1], at_z(3))

    def rs_3(r):
        recv(("rs2", r, 0))
        recv(("rs2", r, 1))
        share = own[r] + rs2[r, 0].astype(F32) + rs2[r, 1].astype(F32)
        own[r] = share
        ssx[0, r : r + 1, :] = jnp.sum(share * share, axis=0, keepdims=True)

    def c_x():
        for d in (1, 3, 2):
            send(("cx", d), cg.at[0, 0], cg.at[0, 4 - d], at_x(d))

    def c_z():
        for d in (1, 3, 2):
            recv(("cx", d))
        for d in (1, 3, 2):
            send(("cz", d), cg.at[0], cg.at[4 - d], at_z(d))

    lane8 = lax.broadcasted_iota(jnp.int32, (8, 128), 1)

    def c_project():
        for d in (1, 3, 2):
            recv(("cz", d))

        def squares(b, total):
            block = cg[b // 4, b % 4].astype(F32)
            block = block * block
            return total + block[0:8] + block[8:16] + block[16:24]

        total = lax.fori_loop(0, 16, squares, jnp.zeros((8, 128), F32))
        factor = lax.rsqrt(jnp.sum(total, axis=-1, keepdims=True) / D + EPS)
        rest = jnp.zeros((8, 128), F32)

        def step(b, total):
            dz, dx = b // 4, b % 4
            head = ((x + dx) % 4) * 4 + (z + dz) % 4
            block = cg[dz, dx].astype(F32)
            row = pl.multiple_of(head * WIDTH, 32)
            for k in range(3):
                gain = gains[pl.ds(head * 3 + k, 1), :]
                part = block[k * 8 : k * 8 + 8] * factor * gain
                part = jnp.concatenate([part, rest], axis=0).astype(BF16)
                if k < 2:
                    total = total + dot(part, wraw[pl.ds(row + k * 128, 128), :])
                else:
                    total = total + dot(part[:, 0:32], wraw[pl.ds(row + 256, 32), :])
            return total

        qkv = lax.fori_loop(0, 16, step, jnp.zeros((16, 512), F32))[0:8]
        angles = table[pl.ds(lengths[y], 8), :]
        other = pltpu.roll(angles, 64, 1)
        front = lane8 < 64
        cosine = jnp.where(front, angles, other)
        sine = jnp.where(front, -other, angles)

        def rotated(value):
            return value * cosine + pltpu.roll(value, 64, 1) * sine

        cq[...] = jnp.concatenate([rotated(qkv[:, 0:128]), rotated(qkv[:, 128:256])], axis=0).astype(BF16)
        ckv[0] = jnp.concatenate([rotated(qkv[:, 256:384]), rest], axis=0).astype(BF16)
        ckv[1] = jnp.concatenate([qkv[:, 384:512], rest], axis=0).astype(BF16)

    def c_attend():
        queries = cq[...]
        length = lengths[y]
        lane = lax.broadcasted_iota(jnp.int32, (16, 128), 1)

        def step(b, carry):
            num, den = carry
            keys = kvg.at[y, b // 8, (b // 2) % 4, b % 2]
            weight = weigh(dot(queries, keys[0:128, :]), lane + key_start(b) < length)
            return num + dot_t(weight.astype(BF16), keys[128:256, :]), den + weight

        zero = jnp.zeros((16, 128), F32)
        num, den = lax.fori_loop(0, 16, step, (zero, zero))
        near = lax.broadcasted_iota(jnp.int32, (16, 16), 1) <= lax.broadcasted_iota(jnp.int32, (16, 16), 0) % 8
        weight = weigh(dot_t(queries, ckv[0]), near)
        num = num + dot(weight.astype(BF16), ckv[1])
        total = jnp.sum(den, axis=-1, keepdims=True) + jnp.sum(weight, axis=-1, keepdims=True)
        result = num / total
        rest = jnp.zeros((8, 128), F32)
        cattg[0, :, 0:128] = jnp.concatenate([result[0:8], rest], axis=0).astype(BF16)
        cattg[0, :, 128:256] = jnp.concatenate([result[8:16], rest], axis=0).astype(BF16)
        for d in (1, 3, 2):
            send(("ca", d), cattg.at[0], cattg.at[4 - d], at_x(d))

    def c_proj():
        for d in (1, 3, 2):
            recv(("ca", d))
        part = dot_t(cattg[0], owt[0])
        for d in range(1, 4):
            part = part + dot_t(cattg[d], owt[d])
        inside = lax.broadcasted_iota(jnp.int32, (16, 384), 1) < WIDTH
        for dz in range(4):
            moved = part if dz == 0 else pltpu.roll(part, SLAB - dz * WIDTH, 1)
            moved = jnp.where(inside, moved[:, 0:384], 0.0)
            if dz:
                cpj[dz] = moved.astype(BF16)
                send(("cr", dz), cpj.at[dz], crs.at[4 - dz], at_z(dz))
            else:
                cown[...] = moved

    def c_sum():
        share = cown[...]
        for d in (1, 3, 2):
            recv(("cr", d))
        for d in range(1, 4):
            share = share + crs[d].astype(F32)
        cown[...] = share
        ssx[0, 8:24, :] = jnp.broadcast_to(jnp.sum(share * share, axis=-1, keepdims=True), (16, 128))

    def finish():
        for d in (1, 3, 2):
            send(("sx", d), ssx.at[0], ssx.at[4 - d], at_x(d))
        for d in (1, 3, 2):
            recv(("sx", d))
        ssz[0] = (ssx[0] + ssx[1]) + (ssx[2] + ssx[3])
        for d in (1, 3, 2):
            send(("sz", d), ssz.at[0], ssz.at[4 - d], at_z(d))
        for d in (1, 3, 2):
            recv(("sz", d))
        factor = lax.rsqrt(((ssz[0] + ssz[1]) + (ssz[2] + ssz[3])) / D + EPS)
        for r in range(ROWS):
            part = own[r] * factor[r : r + 1, :] * pgb[...]
            for k in range(3):
                lo, hi = k * 128, min(k * 128 + 128, WIDTH)
                out[r, :, lo:hi] = (hidden[r, :, lo:hi].astype(F32) + part[lo:hi].T).astype(BF16)
        for k in range(3):
            lo, hi = k * 128, min(k * 128 + 128, WIDTH)
            part = cown[0:4, k * 128 : k * 128 + 128] * factor[8:12, :] * gains[48 + k : 49 + k, :]
            c_out[0, :, lo:hi] = (critique[0, :, lo:hi].astype(F32) + part[:, 0 : hi - lo]).astype(BF16)

    z1(0)
    x1a(0)
    z1(1)
    ow_x()
    c_x()
    x1a(1)
    gain_tables()
    rope_tables()
    e1(0)
    z1(2)
    for copy in fetch_w:
        copy.wait()
    turn_weights(0, 6)
    e2(0)
    x1a(2)
    e1(1)
    z1(3)
    c_z()
    turn_weights(6, 12)
    e2(1)
    x1a(3)
    ow_y1()
    turn_weights(12, 18)
    e1(2)
    c_project()
    e3(0)
    e2(2)
    e1(3)
    ow_y2()
    e4(0)
    project(0)
    kv1(0)
    e3(1)
    e2(3)
    ow_core()
    kv2(0)
    kv3(0)
    e4(1)
    project(1)
    kv1(1)
    e3(2)
    kv4(0)
    ow_turn()
    kv2(1)
    attend(0)
    ax1(0)
    kv3(1)
    e4(2)
    project(2)
    kv1(2)
    e3(3)
    ax2(0)
    kv4(1)
    kv2(2)
    attend(1)
    ax1(1)
    kv3(2)
    proj(0)
    e4(3)
    project(3)
    kv1(3)
    kv4(2)
    rs_2(0)
    ax2(1)
    kv2(3)
    attend(2)
    ax1(2)
    kv3(3)
    proj(1)
    rs_3(0)
    kv4(3)
    ax2(2)
    rs_2(1)
    proj(2)
    attend(3)
    ax1(3)
    rs_3(1)
    c_attend()
    ax2(3)
    rs_2(2)
    proj(3)
    c_proj()
    rs_3(2)
    rs_2(3)
    c_sum()
    rs_3(3)
    finish()
    for copy in copies.values():
        copy.wait_send()


def body(hidden, critique, lengths, pre_gain, post_gain, q_weight, k_weight, v_weight, o_weight):
    pre = jnp.pad(pre_gain.astype(F32).reshape(16, WIDTH), ((0, 0), (0, 384 - WIDTH))).reshape(48, 128)
    post = jnp.pad(post_gain.astype(F32), (0, 384 - WIDTH)).reshape(3, 128)
    gains = jnp.concatenate([pre, post, jnp.zeros((77, 128), F32)], axis=0)
    table = jnp.asarray(rope_table())
    vmem = pl.BlockSpec(memory_space=pltpu.VMEM)
    smem = pl.BlockSpec(memory_space=pltpu.SMEM)
    anywhere = pl.BlockSpec(memory_space=pl.ANY)
    return pl.pallas_call(
        kernel,
        out_shape=(
            jax.ShapeDtypeStruct(hidden.shape, BF16),
            jax.ShapeDtypeStruct(critique.shape, BF16),
        ),
        in_specs=[vmem, vmem, smem, vmem, anywhere, anywhere, anywhere, anywhere, anywhere],
        out_specs=(vmem, vmem),
        scratch_shapes=[
            pltpu.VMEM((ROWS, 4, 4, WIDTH, SPAN), BF16),
            pltpu.VMEM((D, 512), BF16),
            pltpu.VMEM((512, D), BF16),
            pltpu.VMEM((D, 128), F32),
            pltpu.VMEM((WIDTH, 128), F32),
            pltpu.VMEM((D, SPAN), BF16),
            pltpu.VMEM((2056, 128), F32),
            pltpu.VMEM((64, SPAN), F32),
            pltpu.VMEM((64, SPAN), F32),
            pltpu.VMEM((ROWS, 256, HEAD), BF16),
            pltpu.VMEM((ROWS, 2, 4, 2, 256, SPAN), BF16),
            pltpu.VMEM((ROWS, 4, SPAN, 256), BF16),
            pltpu.VMEM((4, 256, SLAB), BF16),
            pltpu.VMEM((4, SLAB, 256), BF16),
            pltpu.VMEM((ROWS, 4, WIDTH, SPAN), BF16),
            pltpu.VMEM((ROWS, WIDTH, SPAN), F32),
            pltpu.VMEM((ROWS, 2, HALF, SPAN), BF16),
            pltpu.VMEM((ROWS, 2, WIDTH, SPAN), BF16),
            pltpu.VMEM((4, 4, 32, 128), BF16),
            pltpu.VMEM((16, 128), BF16),
            pltpu.VMEM((2, 16, 128), BF16),
            pltpu.VMEM((4, 16, 256), BF16),
            pltpu.VMEM((4, 16, 384), BF16),
            pltpu.VMEM((16, 384), F32),
            pltpu.VMEM((4, 16, 384), BF16),
            pltpu.VMEM((4, 24, 128), F32),
            pltpu.VMEM((4, 24, 128), F32),
            pltpu.SemaphoreType.DMA((N_SEM,)),
            pltpu.SemaphoreType.DMA((N_SEM,)),
            pltpu.SemaphoreType.DMA((8,)),
        ],
        compiler_params=pltpu.CompilerParams(
            collective_id=0, has_side_effects=True, vmem_limit_bytes=56 * 1024 * 1024
        ),
        cost_estimate=pl.CostEstimate(flops=5_000_000_000, bytes_accessed=16_000_000, transcendentals=4_000_000),
    )(hidden, critique, lengths, gains, table, q_weight, k_weight, v_weight, o_weight)


def solution(mesh):
    return jax.shard_map(
        body,
        mesh=mesh,
        in_specs=(
            P(None, ("section", "seq"), "head"),
            P("seq", None, "head"),
            P(),
            P(),
            P("head"),
            P(None, "head"),
            P(None, "head"),
            P(None, "head"),
            P("head", None),
        ),
        out_specs=(P(None, ("section", "seq"), "head"), P("seq", None, "head")),
        check_vma=False,
    )
```

time: 510 us -> 143 us (0.28)
  waiting for transfers between devices: 267 us -> 0 us
  Pallas kernels: 0 us -> 135 us
  blocking collectives: 127 us -> 0 us
  matrix products: 37.6 us -> 0 us
  local copies, waits for them, and re-layouts: 30.4 us -> 5.87 us
  other arithmetic: 20.1 us -> 1.4 us
  between operations: 14.1 us -> 0.67 us
  starting transfers between devices: 10.9 us -> 0 us
    pallas_call x0 -> x1, Pallas kernels: none -> 135 us  [body(): pl.pallas_call(kernel, out_shape=(jax.ShapeDtypeStruct(hidden.shape, BF16...]
    reduce_scatter x1 -> x0, waiting for transfers between devices: 99.2 us -> none  [body(): lax.psum_scatter(projected.astype(jnp.bfloat16), 'head', scatter_dimensio...]
    all_gather x3 -> x0, waiting for transfers between devices: 84.6 us -> none  [the longest x1 84.3 us: body(): gathered = lax.all_gather(hidden, 'head', axis=2, tiled=True)]
    all_gather x1 -> x0, blocking collectives: 77.7 us -> none  [body(): features = lax.all_gather(critique, 'head', axis=2, tiled=True)]
    unnamed x6 -> x0, waiting for transfers between devices: 77.7 us -> none
    psum x2 -> x0, blocking collectives: 49.4 us -> none  [the longest x1 43.2 us: body(): share_squares = lax.psum(jnp.sum(share * share, axis=-1), 'head')]
    dot_general x13 -> x0, matrix products: 37.6 us -> none  [the longest x3 9.54 us: partial_sums(): jnp.einsum('rtgjd,rkgd->rtgjk', query_rows, key_rows, preferred_element_t...]
    all_gather x2 -> x0, local copies, waits for them, and re-layouts: 14.1 us -> none  [the longest x1 8.43 us: body(): gathered = lax.all_gather(hidden, 'head', axis=2, tiled=True)]
  transfers between devices with their start and end apart: 7 -> 0, of which waited for: 6 -> 0; matrix products, arithmetic and copies ran while one was open for 12% -> 0% of each run, Pallas kernels for 0% -> 0%
where the time goes in v1:
time: 143 us
  Pallas kernels  135 us (94%)
  local copies, waits for them, and re-layouts  5.87 us (4%)
    pallas_call x1, Pallas kernels, body(): pl.pallas_call(kernel, out_shape=(jax.ShapeDtypeStruct(hidden.shape, BF16...  135 us
    unnamed x2, local copies, waits for them, and re-layouts  3.12 us

profile of v1, /device:TPU:32, one launch (start us, length us, event | category | flops | bytes accessed | tf_op | source)
XLA Modules:
  0.0 142.7 jit_solution(15840723977384469386)
XLA Ops:
  0.6 0.1 pad.14.clone
  0.7 0.7 bitcast_convert_fusion
  1.4 0.8 reshape.20
  2.2 0.7 maximum_maximum_fusion.gains
  2.9 1.9 %copy.12.hidden = bf16[4,128,288]{2,1,0:T(8,128)(2,1)} copy(bf16[4,128,288]{1,2,0:T(8,128)(2,1)} %param.10) | data formatting | bytes 589824 | tf_op args[0]
  4.8 134.8 %shard_map.113 = (bf16[4,128,288]{2,1,0:T(8,128)(2,1)}, bf16[1,4,288]{2,1,0:T(4,128)(2,1)}) custom-call(bf16[4,128,288]{2,1,0:T(8,128)(2,1)} %copy.12.hidden, bf16[1,4,288]{2,1,0:T(4,128)(2,1)} %critique.1, s32[4]{0:T(128)} %lengths.1, f32[128,128]{1,0:T(8,128)} %maximum_maximum_fusion.gains, f32[2056,128]{1,0:T(8,128)} %constant.8.clone.table_hbm, ...), custom_call_target="tpu_custom_call" | custom-call | flops 5000000000 | bytes 16000000 | tf_op jit(solution)/shard_map/pallas_call | solution.py:564
  139.6 1.9 %copy.13 = bf16[4,128,288]{1,2,0:T(8,128)(2,1)} copy(bf16[4,128,288]{2,1,0:T(8,128)(2,1)} %get-tuple-element.2) | data formatting | bytes 589824 | tf_op jit(solution)/shard_map/pallas_call | solution.py:564
  141.4 1.3 copy.15
  (3 shorter events, 0.0 us)

commit v2 on v1

--- a/solution.py
+++ b/solution.py
@@ -26,7 +26,7 @@
 F32 = jnp.float32
 BF16 = jnp.bfloat16
 MESH = pl.DeviceIdType.MESH
-N_SEM = 160
+N_SEM = 192
 
 
 def rope_table():
@@ -46,8 +46,8 @@
 def kernel(
     hidden, critique, lengths, gains, table_hbm, wq, wk, wv, wo,
     out, c_out,
-    xg, wraw, wt, gainb, pgb, xn, table, cosT, sinT, qbuf, kvg, attg, owslab, owt,
-    pb, own, rs1, rs2, cg, cq, ckv, cattg, cpj, cown, crs, ssx, ssz,
+    xg, wraw, wt, pgb, table, cosT, sinT, qbuf, kvg, attg, owslab, owt,
+    pb, own, rs1, rs2, cg, cq, ckv, cattg, cpj, cown, crs, ssx, ssz, prex, prez, fac,
     send_sem, recv_sem, local_sem,
 ):
     s = lax.axis_index("section")
@@ -101,18 +101,22 @@
     fetch_table = fetch(table_hbm, table)
     fetch_o = fetch(wo.at[pl.ds(piece, 32), own_cols], owslab.at[0, pl.ds(piece, 32), :])
 
-    def turn(value):
-        return jnp.concatenate(
-            [value[:, 0:128].T, value[:, 128:256].T, value[:, 256:288].T], axis=0
-        )
-
+    def column(row, k):
+        n = 128 if k < 2 else 32
+        return jnp.broadcast_to(gains[:, k * 128 : k * 128 + 128].T[0:n, row : row + 1], (n, 128))
+
+    gain = jnp.concatenate([column(0, k) for k in range(3)], axis=0)
     for r in range(ROWS):
-        xg[r, 0, 0] = turn(hidden[r].astype(F32)).astype(BF16)
-    c_rows = jnp.concatenate([critique[0].astype(F32), jnp.zeros((4, WIDTH), F32)], axis=0)
-    c_pad = jnp.concatenate([c_rows[:, 256:288], jnp.zeros((8, 96), F32)], axis=1)
-    cg[0, 0] = jnp.concatenate(
-        [c_rows[:, 0:128], c_rows[:, 128:256], c_pad, jnp.zeros((8, 128), F32)], axis=0
-    ).astype(BF16)
+        block = hidden[r].astype(F32)
+        xg[r, x, z] = (block * gain).astype(BF16)
+        prex[0, r : r + 1, :] = jnp.sum(block * block, axis=0, keepdims=True)
+    c_rows = jnp.concatenate([critique[0].astype(F32), jnp.zeros((12, WIDTH), F32)], axis=0)
+    c_sums = jnp.sum(c_rows * c_rows, axis=-1, keepdims=True)
+    prex[0, 4:8, :] = jnp.zeros((4, 128), F32)
+    prex[0, 8:16, :] = jnp.broadcast_to(c_sums[0:8], (8, 128))
+    c_rows = c_rows * gains[0:1, 0:WIDTH]
+    c_last = jnp.concatenate([c_rows[:, 256:288], jnp.zeros((16, 96), F32)], axis=1)
+    cg[0, 0] = jnp.concatenate([c_rows[:, 0:128], c_rows[:, 128:256], c_last], axis=0).astype(BF16)
 
     ssx[0] = jnp.zeros((24, 128), F32)
     partners = [at_x(1), at_x(3), at_x(2), at_z(1), at_z(3), at_z(2), at_y(1), at_y(3), to_zlo, to_core]
@@ -121,33 +125,47 @@
         pl.semaphore_signal(barrier, inc=1, device_id=partner, device_id_type=MESH)
     pl.semaphore_wait(barrier, len(partners))
 
+    zr, zl, zo = (z + 1) % 4, (z + 3) % 4, (z + 2) % 4
+    xr, xl, xo = (x + 1) % 4, (x + 3) % 4, (x + 2) % 4
+    first_half, last_half = pl.ds(0, HALF), pl.ds(HALF, HALF)
+
     def z1(r):
-        send(("z1", r, 0), xg.at[r, 0, 0], xg.at[r, 0, 3], at_z(1))
-        send(("z1", r, 1), xg.at[r, 0, 0], xg.at[r, 0, 1], at_z(3))
+        block = xg.at[r, x, z]
+        send(("z1", r, 0), block, block, at_z(1))
+        send(("z1", r, 1), block, block, at_z(3))
+
+    def x1(r, k, place):
+        block = xg.at[r, x, place]
+        send(("x1", r, k, 0), block, block, at_x(1))
+        send(("x1", r, k, 1), block, block, at_x(3))
 
     def x1a(r):
-        send(("x1a", r, 0), xg.at[r, 0, 0], xg.at[r, 3, 0], at_x(1))
-        send(("x1a", r, 1), xg.at[r, 0, 0], xg.at[r, 1, 0], at_x(3))
+        x1(r, 0, z)
 
     def e1(r):
         recv(("z1", r, 0))
-        send(("z2", r, 0), xg.at[r, 0, 3, 0:HALF], xg.at[r, 0, 2, 0:HALF], at_z(1))
+        half = xg.at[r, x, zl, first_half]
+        send(("z2", r, 0), half, half, at_z(1))
         recv(("z1", r, 1))
-        send(("z2", r, 1), xg.at[r, 0, 1, HALF:WIDTH], xg.at[r, 0, 2, HALF:WIDTH], at_z(3))
+        half = xg.at[r, x, zr, last_half]
+        send(("z2", r, 1), half, half, at_z(3))
+        x1(r, 1, zl)
+        x1(r, 3, zr)
 
     def e2(r):
         recv(("z2", r, 0))
         recv(("z2", r, 1))
-        send(("x1b", r, 0), xg.at[r, 0, 1:4], xg.at[r, 3, 1:4], at_x(1))
-        send(("x1b", r, 1), xg.at[r, 0, 1:4], xg.at[r, 1, 1:4], at_x(3))
+        x1(r, 2, zo)
 
     def e3(r):
-        recv(("x1a", r, 0))
-        recv(("x1b", r, 0))
-        send(("x2", r, 0), xg.at[r, 3, :, 0:HALF], xg.at[r, 2, :, 0:HALF], at_x(1))
-        recv(("x1a", r, 1))
-        recv(("x1b", r, 1))
-        send(("x2", r, 1), xg.at[r, 1, :, HALF:WIDTH], xg.at[r, 2, :, HALF:WIDTH], at_x(3))
+        for k in range(4):
+            recv(("x1", r, k, 0))
+        half = xg.at[r, xl, :, first_half]
+        send(("x2", r, 0), half, half, at_x(1))
+        for k in range(4):
+            recv(("x1", r, k, 1))
+        half = xg.at[r, xr, :, last_half]
+        send(("x2", r, 1), half, half, at_x(3))
 
     def e4(r):
         recv(("x2", r, 0))
@@ -193,15 +211,8 @@
         lax.fori_loop(0, 4, step, 0)
 
     def gain_tables():
-        turned = gains[...].T
-        for hh in range(16):
-            for k in range(3):
-                n = 128 if k < 2 else 32
-                column = turned[0:n, hh * 3 + k : hh * 3 + k + 1]
-                gainb[hh * WIDTH + k * 128 : hh * WIDTH + k * 128 + n, :] = jnp.broadcast_to(column, (n, 128))
         for k in range(3):
-            n = 128 if k < 2 else 32
-            pgb[k * 128 : k * 128 + n, :] = jnp.broadcast_to(turned[0:n, 48 + k : 49 + k], (n, 128))
+            pgb[k * 128 : min(k * 128 + 128, WIDTH), :] = column(1, k)
 
     def rope_tables():
         fetch_table.wait()
@@ -218,25 +229,24 @@
 
         lax.fori_loop(lo, hi, step, 0)
 
-    def source_head(b):
-        return ((x + b // 4) % 4) * 4 + (z + b % 4) % 4
+    def pre_x():
+        for d in (1, 3, 2):
+            send(("px", d), prex.at[0], prex.at[4 - d], at_x(d))
+
+    def pre_z():
+        for d in (1, 3, 2):
+            recv(("px", d))
+        prez[0] = (prex[0] + prex[1]) + (prex[2] + prex[3])
+        for d in (1, 3, 2):
+            send(("pz", d), prez.at[0], prez.at[4 - d], at_z(d))
+
+    def pre_done():
+        for d in (1, 3, 2):
+            recv(("pz", d))
+        fac[...] = lax.rsqrt(((prez[0] + prez[1]) + (prez[2] + prez[3])) / D + EPS)
 
     def project(r):
-        def squares(b, total):
-            block = xg[r, b // 4, b % 4].astype(F32)
-            return total + jnp.sum((block * block).reshape(WIDTH // 8, 8, 128), axis=0)
-
-        total = lax.fori_loop(0, 16, squares, jnp.zeros((8, 128), F32))
-        factor = lax.rsqrt(jnp.sum(total, axis=0, keepdims=True) / D + EPS)
-
-        def scale(b, carry):
-            rows = pl.ds(pl.multiple_of(source_head(b) * WIDTH, 32), WIDTH)
-            block = xg[r, b // 4, b % 4].astype(F32)
-            xn[rows, :] = (block * factor * gainb[rows, :]).astype(BF16)
-            return carry
-
-        lax.fori_loop(0, 16, scale, 0)
-        qkv = dot(wt[...], xn[...])
+        qkv = dot(wt[...], xg[r].reshape(D, SPAN)) * fac[r : r + 1, :]
         cosine, sine = cosT[...], sinT[...]
 
         def rotated(value):
@@ -287,12 +297,15 @@
 
         def step(b, carry):
             num, den = carry
-            keys = kvg.at[r, b // 8, (b // 2) % 4, b % 2]
-            weight = weigh(dot(queries, keys[0:128, :]), lane + key_start(b) <= limit)
-            return num + dot_t(weight.astype(BF16), keys[128:256, :]), den + weight
+            for i in range(4):
+                keys = kvg.at[r, b // 2, (b % 2) * 2 + i // 2, i % 2]
+                weight = weigh(dot(queries, keys[0:128, :]), lane + key_start(b * 4 + i) <= limit)
+                num = num + dot_t(weight.astype(BF16), keys[128:256, :])
+                den = den + weight
+            return num, den
 
         zero = jnp.zeros((256, 128), F32)
-        num, den = lax.fori_loop(0, 16, step, (zero, zero))
+        num, den = lax.fori_loop(0, 4, step, (zero, zero))
         result = num / jnp.sum(den, axis=-1, keepdims=True)
         attg[r, 0, :, 0:128] = result[0:128].astype(BF16)
         attg[r, 0, :, 128:256] = result[128:256].astype(BF16)
@@ -354,31 +367,17 @@
         for d in (1, 3, 2):
             recv(("cz", d))
 
-        def squares(b, total):
-            block = cg[b // 4, b % 4].astype(F32)
-            block = block * block
-            return total + block[0:8] + block[8:16] + block[16:24]
-
-        total = lax.fori_loop(0, 16, squares, jnp.zeros((8, 128), F32))
-        factor = lax.rsqrt(jnp.sum(total, axis=-1, keepdims=True) / D + EPS)
+        def step(dz, total):
+            for dx in range(4):
+                head = ((x + dx) % 4) * 4 + (z + dz) % 4
+                row = pl.multiple_of(head * WIDTH, 32)
+                total = total + dot(cg[dz, dx, 0:16], wraw[pl.ds(row, 128), :])
+                total = total + dot(cg[dz, dx, 16:32], wraw[pl.ds(row + 128, 128), :])
+                total = total + dot(cg[dz, dx, 32:48, 0:32], wraw[pl.ds(row + 256, 32), :])
+            return total
+
+        qkv = lax.fori_loop(0, 4, step, jnp.zeros((16, 512), F32))[0:8] * fac[8:16, 0:1]
         rest = jnp.zeros((8, 128), F32)
-
-        def step(b, total):
-            dz, dx = b // 4, b % 4
-            head = ((x + dx) % 4) * 4 + (z + dz) % 4
-            block = cg[dz, dx].astype(F32)
-            row = pl.multiple_of(head * WIDTH, 32)
-            for k in range(3):
-                gain = gains[pl.ds(head * 3 + k, 1), :]
-                part = block[k * 8 : k * 8 + 8] * factor * gain
-                part = jnp.concatenate([part, rest], axis=0).astype(BF16)
-                if k < 2:
-                    total = total + dot(part, wraw[pl.ds(row + k * 128, 128), :])
-                else:
-                    total = total + dot(part[:, 0:32], wraw[pl.ds(row + 256, 32), :])
-            return total
-
-        qkv = lax.fori_loop(0, 16, step, jnp.zeros((16, 512), F32))[0:8]
         angles = table[pl.ds(lengths[y], 8), :]
         other = pltpu.roll(angles, 64, 1)
         front = lane8 < 64
@@ -397,14 +396,13 @@
         length = lengths[y]
         lane = lax.broadcasted_iota(jnp.int32, (16, 128), 1)
 
-        def step(b, carry):
-            num, den = carry
+        num = jnp.zeros((16, 128), F32)
+        den = jnp.zeros((16, 128), F32)
+        for b in range(16):
             keys = kvg.at[y, b // 8, (b // 2) % 4, b % 2]
             weight = weigh(dot(queries, keys[0:128, :]), lane + key_start(b) < length)
-            return num + dot_t(weight.astype(BF16), keys[128:256, :]), den + weight
-
-        zero = jnp.zeros((16, 128), F32)
-        num, den = lax.fori_loop(0, 16, step, (zero, zero))
+            num = num + dot_t(weight.astype(BF16), keys[128:256, :])
+            den = den + weight
         near = lax.broadcasted_iota(jnp.int32, (16, 16), 1) <= lax.broadcasted_iota(jnp.int32, (16, 16), 0) % 8
         weight = weigh(dot_t(queries, ckv[0]), near)
         num = num + dot(weight.astype(BF16), ckv[1])
@@ -454,19 +452,18 @@
         factor = lax.rsqrt(((ssz[0] + ssz[1]) + (ssz[2] + ssz[3])) / D + EPS)
         for r in range(ROWS):
             part = own[r] * factor[r : r + 1, :] * pgb[...]
-            for k in range(3):
-                lo, hi = k * 128, min(k * 128 + 128, WIDTH)
-                out[r, :, lo:hi] = (hidden[r, :, lo:hi].astype(F32) + part[lo:hi].T).astype(BF16)
+            out[r] = (hidden[r].astype(F32) + part).astype(BF16)
         for k in range(3):
             lo, hi = k * 128, min(k * 128 + 128, WIDTH)
-            part = cown[0:4, k * 128 : k * 128 + 128] * factor[8:12, :] * gains[48 + k : 49 + k, :]
+            part = cown[0:4, k * 128 : k * 128 + 128] * factor[8:12, :] * gains[1:2, k * 128 : k * 128 + 128]
             c_out[0, :, lo:hi] = (critique[0, :, lo:hi].astype(F32) + part[:, 0 : hi - lo]).astype(BF16)
 
+    pre_x()
     z1(0)
     x1a(0)
+    c_x()
     z1(1)
     ow_x()
-    c_x()
     x1a(1)
     gain_tables()
     rope_tables()
@@ -479,6 +476,7 @@
     x1a(2)
     e1(1)
     z1(3)
+    pre_z()
     c_z()
     turn_weights(6, 12)
     e2(1)
@@ -486,8 +484,9 @@
     ow_y1()
     turn_weights(12, 18)
     e1(2)
+    pre_done()
+    e3(0)
     c_project()
-    e3(0)
     e2(2)
     e1(3)
     ow_y2()
@@ -554,17 +553,17 @@
 
 
 def body(hidden, critique, lengths, pre_gain, post_gain, q_weight, k_weight, v_weight, o_weight):
-    pre = jnp.pad(pre_gain.astype(F32).reshape(16, WIDTH), ((0, 0), (0, 384 - WIDTH))).reshape(48, 128)
-    post = jnp.pad(post_gain.astype(F32), (0, 384 - WIDTH)).reshape(3, 128)
-    gains = jnp.concatenate([pre, post, jnp.zeros((77, 128), F32)], axis=0)
+    own_gain = lax.dynamic_slice(pre_gain, (lax.axis_index("head") * WIDTH,), (WIDTH,))
+    gains = jnp.pad(jnp.stack([own_gain, post_gain]).astype(F32), ((0, 6), (0, 384 - WIDTH)))
     table = jnp.asarray(rope_table())
     vmem = pl.BlockSpec(memory_space=pltpu.VMEM)
     smem = pl.BlockSpec(memory_space=pltpu.SMEM)
     anywhere = pl.BlockSpec(memory_space=pl.ANY)
-    return pl.pallas_call(
+    turned = jnp.transpose(hidden, (0, 2, 1))
+    result, c_result = pl.pallas_call(
         kernel,
         out_shape=(
-            jax.ShapeDtypeStruct(hidden.shape, BF16),
+            jax.ShapeDtypeStruct(turned.shape, BF16),
             jax.ShapeDtypeStruct(critique.shape, BF16),
         ),
         in_specs=[vmem, vmem, smem, vmem, anywhere, anywhere, anywhere, anywhere, anywhere],
@@ -573,9 +572,7 @@
             pltpu.VMEM((ROWS, 4, 4, WIDTH, SPAN), BF16),
             pltpu.VMEM((D, 512), BF16),
             pltpu.VMEM((512, D), BF16),
-            pltpu.VMEM((D, 128), F32),
             pltpu.VMEM((WIDTH, 128), F32),
-            pltpu.VMEM((D, SPAN), BF16),
             pltpu.VMEM((2056, 128), F32),
             pltpu.VMEM((64, SPAN), F32),
             pltpu.VMEM((64, SPAN), F32),
@@ -588,7 +585,7 @@
             pltpu.VMEM((ROWS, WIDTH, SPAN), F32),
             pltpu.VMEM((ROWS, 2, HALF, SPAN), BF16),
             pltpu.VMEM((ROWS, 2, WIDTH, SPAN), BF16),
-            pltpu.VMEM((4, 4, 32, 128), BF16),
+            pltpu.VMEM((4, 4, 48, 128), BF16),
             pltpu.VMEM((16, 128), BF16),
             pltpu.VMEM((2, 16, 128), BF16),
             pltpu.VMEM((4, 16, 256), BF16),
@@ -597,6 +594,9 @@
             pltpu.VMEM((4, 16, 384), BF16),
             pltpu.VMEM((4, 24, 128), F32),
             pltpu.VMEM((4, 24, 128), F32),
+            pltpu.VMEM((4, 16, 128), F32),
+            pltpu.VMEM((4, 16, 128), F32),
+            pltpu.VMEM((16, 128), F32),
             pltpu.SemaphoreType.DMA((N_SEM,)),
             pltpu.SemaphoreType.DMA((N_SEM,)),
             pltpu.SemaphoreType.DMA((8,)),
@@ -605,7 +605,8 @@
             collective_id=0, has_side_effects=True, vmem_limit_bytes=56 * 1024 * 1024
         ),
         cost_estimate=pl.CostEstimate(flops=5_000_000_000, bytes_accessed=16_000_000, transcendentals=4_000_000),
-    )(hidden, critique, lengths, gains, table, q_weight, k_weight, v_weight, o_weight)
+    )(turned, critique, lengths, gains, table, q_weight, k_weight, v_weight, o_weight)
+    return jnp.transpose(result, (0, 2, 1)), c_result
 
 
 def solution(mesh):

time: 143 us -> 129 us (0.902)
  Pallas kernels: 135 us -> 122 us
  local copies, waits for them, and re-layouts: 5.87 us -> 4.41 us
    pallas_call x1, Pallas kernels: 135 us -> 122 us  [body(): pl.pallas_call(kernel, out_shape=(jax.ShapeDtypeStruct(turned.shape, BF16...]
    pallas_call x1 -> x0, local copies, waits for them, and re-layouts: 1.88 us -> none  [body(): pl.pallas_call(kernel, out_shape=(jax.ShapeDtypeStruct(hidden.shape, BF16...]
where the time goes in v2:
time: 129 us; the launch traced here: 128 us
  Pallas kernels  122 us (95%)
  local copies, waits for them, and re-layouts  4.41 us (3%)
    pallas_call x1, Pallas kernels, body(): pl.pallas_call(kernel, out_shape=(jax.ShapeDtypeStruct(turned.shape, BF16...  122 us
    unnamed x2, local copies, waits for them, and re-layouts  2.95 us

profile of v2, /device:TPU:32, one launch (start us, length us, event | category | flops | bytes accessed | tf_op | source)
XLA Modules:
  0.0 127.8 jit_solution(11877500788778317363)
XLA Ops:
  0.6 0.8 dynamic_slice.3
  1.4 0.7 stack.10
  2.1 0.6 fusion.6.gains
  2.7 122.2 %shard_map.113 = (bf16[4,288,128]{2,1,0:T(8,128)(2,1)}, bf16[1,4,288]{2,1,0:T(4,128)(2,1)}) custom-call(bf16[4,288,128]{2,1,0:T(8,128)(2,1)} %bitcast.3, bf16[1,4,288]{2,1,0:T(4,128)(2,1)} %critique.1, s32[4]{0:T(128)} %lengths.1, f32[8,384]{1,0:T(8,128)} %fusion.6.gains, f32[2056,128]{1,0:T(8,128)} %constant.15.clone.table_hbm, bf16[4608,256]{1,0:T(8,128)(2,1)} %wq.1, ...), custom_call_target="tpu_custom_call" | custom-call | flops 5000000000 | bytes 16000000 | tf_op jit(solution)/shard_map/pallas_call | solution.py:563
  124.9 1.7 %copy.14 = bf16[4,128,288]{1,2,0:T(8,128)(2,1)} copy(bf16[4,128,288]{1,2,0:T(8,128)(2,1)} %bitcast.2) | data formatting | bytes 589824
  126.6 1.3 copy.15
  (1 shorter events, 0.0 us)

commit v3 on v2

--- a/solution.py
+++ b/solution.py
@@ -17,6 +17,7 @@
 WIDTH = 288
 SLAB = 4 * WIDTH
 HALF = WIDTH // 2
+FIRST = 240
 STEPS = 4
 
 EPS = 1e-06
@@ -26,7 +27,7 @@
 F32 = jnp.float32
 BF16 = jnp.bfloat16
 MESH = pl.DeviceIdType.MESH
-N_SEM = 192
+N_SEM = 232
 
 
 def rope_table():
@@ -68,6 +69,11 @@
     to_zlo = {"section": (1 - zlo) * 2 + core}
     to_core = {"section": zlo * 2 + 1 - core}
 
+    partners = [at_x(1), at_x(3), at_x(2), at_z(1), at_z(3), at_z(2), at_y(1), at_y(3), to_zlo, to_core]
+    barrier = pltpu.get_barrier_semaphore()
+    for partner in partners:
+        pl.semaphore_signal(barrier, inc=1, device_id=partner, device_id_type=MESH)
+
     copies = {}
 
     def send(name, src, dst, device):
@@ -119,36 +125,34 @@
     cg[0, 0] = jnp.concatenate([c_rows[:, 0:128], c_rows[:, 128:256], c_last], axis=0).astype(BF16)
 
     ssx[0] = jnp.zeros((24, 128), F32)
-    partners = [at_x(1), at_x(3), at_x(2), at_z(1), at_z(3), at_z(2), at_y(1), at_y(3), to_zlo, to_core]
-    barrier = pltpu.get_barrier_semaphore()
-    for partner in partners:
-        pl.semaphore_signal(barrier, inc=1, device_id=partner, device_id_type=MESH)
     pl.semaphore_wait(barrier, len(partners))
 
     zr, zl, zo = (z + 1) % 4, (z + 3) % 4, (z + 2) % 4
     xr, xl, xo = (x + 1) % 4, (x + 3) % 4, (x + 2) % 4
-    first_half, last_half = pl.ds(0, HALF), pl.ds(HALF, HALF)
+    main = pl.ds(0, FIRST)
+    main_up, main_down = pl.ds(0, 128), pl.ds(128, FIRST - 128)
+    rest = pl.ds(FIRST, WIDTH - FIRST)
+    rest_up, rest_down = pl.ds(FIRST, 16), pl.ds(FIRST + 16, WIDTH - FIRST - 16)
+
+    def pair_send(name, up, down, where):
+        send(name + (0,), up, up, where(1))
+        send(name + (1,), down, down, where(3))
 
     def z1(r):
-        block = xg.at[r, x, z]
-        send(("z1", r, 0), block, block, at_z(1))
-        send(("z1", r, 1), block, block, at_z(3))
+        block = xg.at[r, x, z, main]
+        pair_send(("z1", r), block, block, at_z)
 
     def x1(r, k, place):
-        block = xg.at[r, x, place]
-        send(("x1", r, k, 0), block, block, at_x(1))
-        send(("x1", r, k, 1), block, block, at_x(3))
+        block = xg.at[r, x, place, main]
+        pair_send(("x1", r, k), block, block, at_x)
 
     def x1a(r):
         x1(r, 0, z)
 
     def e1(r):
         recv(("z1", r, 0))
-        half = xg.at[r, x, zl, first_half]
-        send(("z2", r, 0), half, half, at_z(1))
         recv(("z1", r, 1))
-        half = xg.at[r, x, zr, last_half]
-        send(("z2", r, 1), half, half, at_z(3))
+        pair_send(("z2", r), xg.at[r, x, zl, main_up], xg.at[r, x, zr, main_down], at_z)
         x1(r, 1, zl)
         x1(r, 3, zr)
 
@@ -160,16 +164,33 @@
     def e3(r):
         for k in range(4):
             recv(("x1", r, k, 0))
-        half = xg.at[r, xl, :, first_half]
-        send(("x2", r, 0), half, half, at_x(1))
-        for k in range(4):
             recv(("x1", r, k, 1))
-        half = xg.at[r, xr, :, last_half]
-        send(("x2", r, 1), half, half, at_x(3))
+        pair_send(("x2", r), xg.at[r, xl, :, main_up], xg.at[r, xr, :, main_down], at_x)
+
+    def b1(r):
+        block = xg.at[r, x, z, rest]
+        pair_send(("b1", r), block, block, at_x)
+
+    def b2(r):
+        recv(("b1", r, 0))
+        recv(("b1", r, 1))
+        pair_send(("b2", r), xg.at[r, xl, z, rest_up], xg.at[r, xr, z, rest_down], at_x)
+
+    def b3(r):
+        recv(("b2", r, 0))
+        recv(("b2", r, 1))
+        block = xg.at[r, :, z, rest]
+        pair_send(("b3", r), block, block, at_z)
+
+    def b4(r):
+        recv(("b3", r, 0))
+        recv(("b3", r, 1))
+        pair_send(("b4", r), xg.at[r, :, zl, rest_up], xg.at[r, :, zr, rest_down], at_z)
 
     def e4(r):
-        recv(("x2", r, 0))
-        recv(("x2", r, 1))
+        for part in ("x2", "b4"):
+            recv((part, r, 0))
+            recv((part, r, 1))
 
     def ow_x():
         for d in (1, 3, 2):
@@ -221,6 +242,10 @@
         cosT[...] = turned[0:64]
         sinT[...] = turned[64:128]
 
+    def fetch_weights():
+        for copy in fetch_w:
+            copy.wait()
+
     def turn_weights(lo, hi):
         def step(c, carry):
             row = pl.multiple_of(c * 256, 256)
@@ -258,24 +283,43 @@
         kvg[r, 0, 0, 0, 0:128, :] = rotated(qkv[256:384]).astype(BF16)
         kvg[r, 0, 0, 0, 128:256, :] = qkv[384:512].astype(BF16)
 
-    def kv1(r):
-        send(("kv1", r), kvg.at[r, 0, 0, 0], kvg.at[r, 0, 0, 1], to_zlo)
-
-    def kv2(r):
-        recv(("kv1", r))
-        send(("kv2", r, 0), kvg.at[r, 0, 0], kvg.at[r, 0, 3], at_y(1))
-        send(("kv2", r, 1), kvg.at[r, 0, 0], kvg.at[r, 0, 1], at_y(3))
-
-    def kv3(r):
-        recv(("kv2", r, 0))
-        send(("kv3", r, 0), kvg.at[r, 0, 3, 0], kvg.at[r, 0, 2, 0], at_y(1))
-        recv(("kv2", r, 1))
-        send(("kv3", r, 1), kvg.at[r, 0, 1, 1], kvg.at[r, 0, 2, 1], at_y(3))
-
-    def kv4(r):
-        recv(("kv3", r, 0))
-        recv(("kv3", r, 1))
-        send(("kv4", r), kvg.at[r, 0], kvg.at[r, 1], to_core)
+    def kv_core(r, dy):
+        send(("kvc", r, dy), kvg.at[r, 0, dy], kvg.at[r, 1, dy], to_core)
+
+    def kv_y(name, r, dz):
+        send((name, r, 0), kvg.at[r, 0, 0, dz], kvg.at[r, 0, 3, dz], at_y(1))
+        send((name, r, 1), kvg.at[r, 0, 0, dz], kvg.at[r, 0, 1, dz], at_y(3))
+
+    def kv_on(name, r, dz):
+        send((name, r, 0), kvg.at[r, 0, 3, dz, 0:128], kvg.at[r, 0, 2, dz, 0:128], at_y(1))
+        send((name, r, 1), kvg.at[r, 0, 1, dz, 128:256], kvg.at[r, 0, 2, dz, 128:256], at_y(3))
+
+    def kva(r):
+        send(("kvz", r), kvg.at[r, 0, 0, 0], kvg.at[r, 0, 0, 1], to_zlo)
+        kv_y("kvy1", r, 0)
+
+    def kvb(r):
+        recv(("kvz", r))
+        kv_y("kvy2", r, 1)
+        kv_core(r, 0)
+
+    def kvc(r):
+        recv(("kvy1", r, 0))
+        recv(("kvy1", r, 1))
+        kv_on("kvy3", r, 0)
+
+    def kvd(r):
+        recv(("kvy2", r, 0))
+        recv(("kvy2", r, 1))
+        kv_on("kvy4", r, 1)
+        kv_core(r, 1)
+        kv_core(r, 3)
+
+    def kve(r):
+        for name in ("kvy3", "kvy4"):
+            recv((name, r, 0))
+            recv((name, r, 1))
+        kv_core(r, 2)
 
     def key_start(b):
         dc, dy, dz = b // 8, (b // 2) % 4, b % 2
@@ -286,14 +330,15 @@
         capped = CAP * jnp.tanh(scores * (SCALE / CAP))
         return jnp.where(keep, jnp.exp(capped), 0.0)
 
-    def attend(r):
-        recv(("kv4", r))
-        queries = qbuf[r]
+    def attend(r, j):
+        if j == 0:
+            for dy in range(4):
+                recv(("kvc", r, dy))
+        queries = qbuf[r, j * 128 : j * 128 + 128, :]
         length = lengths[r]
-        first = (s * 4 + y) * SPAN
-        token = first + lax.broadcasted_iota(jnp.int32, (256, 128), 0) % SPAN
+        token = (s * 4 + y) * SPAN + lax.broadcasted_iota(jnp.int32, (128, 128), 0)
         limit = jnp.minimum(token, length - 1)
-        lane = lax.broadcasted_iota(jnp.int32, (256, 128), 1)
+        lane = lax.broadcasted_iota(jnp.int32, (128, 128), 1)
 
         def step(b, carry):
             num, den = carry
@@ -304,49 +349,54 @@
                 den = den + weight
             return num, den
 
-        zero = jnp.zeros((256, 128), F32)
+        zero = jnp.zeros((128, 128), F32)
         num, den = lax.fori_loop(0, 4, step, (zero, zero))
-        result = num / jnp.sum(den, axis=-1, keepdims=True)
-        attg[r, 0, :, 0:128] = result[0:128].astype(BF16)
-        attg[r, 0, :, 128:256] = result[128:256].astype(BF16)
-
-    def ax1(r):
-        send(("ax1", r, 0), attg.at[r, 0], attg.at[r, 3], at_x(1))
-        send(("ax1", r, 1), attg.at[r, 0], attg.at[r, 1], at_x(3))
-
-    def ax2(r):
-        recv(("ax1", r, 0))
-        send(("ax2", r, 0), attg.at[r, 3, 0:64], attg.at[r, 2, 0:64], at_x(1))
-        recv(("ax1", r, 1))
-        send(("ax2", r, 1), attg.at[r, 1, 64:128], attg.at[r, 2, 64:128], at_x(3))
+        attg[r, 0, j] = (num / jnp.sum(den, axis=-1, keepdims=True)).astype(BF16)
+        send(("ax1", r, j, 0), attg.at[r, 0, j], attg.at[r, 3, j], at_x(1))
+        send(("ax1", r, j, 1), attg.at[r, 0, j], attg.at[r, 1, j], at_x(3))
+
+    def ax2(r, j):
+        recv(("ax1", r, j, 0))
+        recv(("ax1", r, j, 1))
+        send(("ax2", r, j, 0), attg.at[r, 3, j, 0:64], attg.at[r, 2, j, 0:64], at_x(1))
+        send(("ax2", r, j, 1), attg.at[r, 1, j, 64:128], attg.at[r, 2, j, 64:128], at_x(3))
+
+    low, high = pl.ds(0, HALF), pl.ds(HALF, HALF)
 
     def proj(r):
-        recv(("ax2", r, 0))
-        recv(("ax2", r, 1))
+        for j in range(2):
+            recv(("ax2", r, j, 0))
+            recv(("ax2", r, j, 1))
+        attended = [jnp.concatenate([attg[r, d, 0], attg[r, d, 1]], axis=1) for d in range(4)]
         for dz in (2, 1, 3, 0):
             rows = pl.ds(dz * WIDTH, WIDTH)
-            part = dot_t(owt[0, rows, :], attg[r, 0])
+            part = dot_t(owt[0, rows, :], attended[0])
             for d in range(1, 4):
-                part = part + dot_t(owt[d, rows, :], attg[r, d])
+                part = part + dot_t(owt[d, rows, :], attended[d])
             if dz:
                 pb[r, dz] = part.astype(BF16)
             else:
                 own[r] = part
             if dz == 2:
-                send(("rs1", r, 0), pb.at[r, 2, 0:HALF], rs1.at[r, 0], at_z(1))
-                send(("rs1", r, 1), pb.at[r, 2, HALF:WIDTH], rs1.at[r, 1], at_z(3))
+                send(("rs1", r, 0), pb.at[r, 2, low], rs1.at[r, 0], at_z(1))
+                send(("rs1", r, 1), pb.at[r, 2, high], rs1.at[r, 1], at_z(3))
+            if dz == 1:
+                send(("rs2", r, 0), pb.at[r, 1, high], rs2.at[r, 0, high], at_z(1))
+            if dz == 3:
+                send(("rs2", r, 1), pb.at[r, 3, low], rs2.at[r, 1, low], at_z(3))
 
     def rs_2(r):
         recv(("rs1", r, 0))
         pb[r, 1, 0:HALF] = (pb[r, 1, 0:HALF].astype(F32) + rs1[r, 0].astype(F32)).astype(BF16)
-        send(("rs2", r, 0), pb.at[r, 1], rs2.at[r, 0], at_z(1))
+        send(("rs3", r, 0), pb.at[r, 1, low], rs2.at[r, 0, low], at_z(1))
         recv(("rs1", r, 1))
         pb[r, 3, HALF:WIDTH] = (pb[r, 3, HALF:WIDTH].astype(F32) + rs1[r, 1].astype(F32)).astype(BF16)
-        send(("rs2", r, 1), pb.at[r, 3], rs2.at[r, 1], at_z(3))
+        send(("rs3", r, 1), pb.at[r, 3, high], rs2.at[r, 1, high], at_z(3))
 
     def rs_3(r):
-        recv(("rs2", r, 0))
-        recv(("rs2", r, 1))
+        for name in ("rs2", "rs3"):
+            recv((name, r, 0))
+            recv((name, r, 1))
         share = own[r] + rs2[r, 0].astype(F32) + rs2[r, 1].astype(F32)
         own[r] = share
         ssx[0, r : r + 1, :] = jnp.sum(share * share, axis=0, keepdims=True)
@@ -439,14 +489,18 @@
         cown[...] = share
         ssx[0, 8:24, :] = jnp.broadcast_to(jnp.sum(share * share, axis=-1, keepdims=True), (16, 128))
 
-    def finish():
+    def sum_x():
         for d in (1, 3, 2):
             send(("sx", d), ssx.at[0], ssx.at[4 - d], at_x(d))
+
+    def sum_z():
         for d in (1, 3, 2):
             recv(("sx", d))
         ssz[0] = (ssx[0] + ssx[1]) + (ssx[2] + ssx[3])
         for d in (1, 3, 2):
             send(("sz", d), ssz.at[0], ssz.at[4 - d], at_z(d))
+
+    def finish():
         for d in (1, 3, 2):
             recv(("sz", d))
         factor = lax.rsqrt(((ssz[0] + ssz[1]) + (ssz[2] + ssz[3])) / D + EPS)
@@ -458,95 +512,120 @@
             part = cown[0:4, k * 128 : k * 128 + 128] * factor[8:12, :] * gains[1:2, k * 128 : k * 128 + 128]
             c_out[0, :, lo:hi] = (critique[0, :, lo:hi].astype(F32) + part[:, 0 : hi - lo]).astype(BF16)
 
+    z1(0)
+    c_x()
+    b1(0)
+    x1a(0)
+    b1(1)
+    b1(3)
     pre_x()
-    z1(0)
-    x1a(0)
-    c_x()
+    rope_tables()
+    fetch_weights()
+    turn_weights(0, 6)
+    c_z()
+    b2(0)
+    x1a(1)
+    ow_x()
+    gain_tables()
+    turn_weights(6, 12)
+    turn_weights(12, 18)
+    b2(1)
+    b2(3)
+    e1(0)
+    b3(0)
+    z1(2)
+    pre_z()
+    b1(2)
     z1(1)
-    ow_x()
-    x1a(1)
-    gain_tables()
-    rope_tables()
-    e1(0)
-    z1(2)
-    for copy in fetch_w:
-        copy.wait()
-    turn_weights(0, 6)
+    ow_y1()
     e2(0)
     x1a(2)
+    b4(0)
+    b2(2)
+    e3(0)
+    e1(2)
+    b3(2)
+    pre_done()
+    c_project()
+    ow_y2()
     e1(1)
+    b3(1)
     z1(3)
-    pre_z()
-    c_z()
-    turn_weights(6, 12)
-    e2(1)
-    x1a(3)
-    ow_y1()
-    turn_weights(12, 18)
-    e1(2)
-    pre_done()
-    e3(0)
-    c_project()
-    e2(2)
-    e1(3)
-    ow_y2()
     e4(0)
     project(0)
-    kv1(0)
+    kva(0)
+    e2(2)
+    ow_core()
+    b4(2)
+    kvc(0)
+    e2(1)
+    e3(2)
+    x1a(3)
+    kvb(0)
+    b4(1)
     e3(1)
+    kvd(0)
+    e1(3)
+    b3(3)
+    kve(0)
+    e4(2)
+    project(2)
+    kva(2)
+    ow_turn()
     e2(3)
-    ow_core()
-    kv2(0)
-    kv3(0)
+    attend(0, 0)
     e4(1)
     project(1)
-    kv1(1)
-    e3(2)
-    kv4(0)
-    ow_turn()
-    kv2(1)
-    attend(0)
-    ax1(0)
-    kv3(1)
-    e4(2)
-    project(2)
-    kv1(2)
+    kvb(2)
+    kvc(2)
+    attend(0, 1)
+    kva(1)
+    b4(3)
     e3(3)
-    ax2(0)
-    kv4(1)
-    kv2(2)
-    attend(1)
-    ax1(1)
-    kv3(2)
-    proj(0)
+    ax2(0, 0)
+    kvd(2)
+    ax2(0, 1)
+    kvb(1)
+    kvc(1)
+    kve(2)
     e4(3)
     project(3)
-    kv1(3)
-    kv4(2)
+    kvd(1)
+    kva(3)
+    attend(2, 0)
+    attend(2, 1)
+    kve(1)
+    proj(0)
+    ax2(2, 0)
+    kvb(3)
+    kvc(3)
+    attend(1, 0)
+    ax2(2, 1)
+    attend(1, 1)
     rs_2(0)
-    ax2(1)
-    kv2(3)
-    attend(2)
-    ax1(2)
-    kv3(3)
+    kvd(3)
+    ax2(1, 0)
+    proj(2)
+    ax2(1, 1)
+    kve(3)
+    rs_3(0)
     proj(1)
-    rs_3(0)
-    kv4(3)
-    ax2(2)
+    attend(3, 0)
+    rs_2(2)
+    attend(3, 1)
+    c_attend()
+    ax2(3, 0)
     rs_2(1)
-    proj(2)
-    attend(3)
-    ax1(3)
+    ax2(3, 1)
+    c_proj()
+    proj(3)
+    rs_3(2)
     rs_3(1)
-    c_attend()
-    ax2(3)
-    rs_2(2)
-    proj(3)
-    c_proj()
-    rs_3(2)
+    c_sum()
     rs_2(3)
-    c_sum()
     rs_3(3)
+    sum_x()
+    sum_z()
     finish()
     for copy in copies.values():
         copy.wait_send()
@@ -578,7 +657,7 @@
             pltpu.VMEM((64, SPAN), F32),
             pltpu.VMEM((ROWS, 256, HEAD), BF16),
             pltpu.VMEM((ROWS, 2, 4, 2, 256, SPAN), BF16),
-            pltpu.VMEM((ROWS, 4, SPAN, 256), BF16),
+            pltpu.VMEM((ROWS, 4, 2, SPAN, HEAD), BF16),
             pltpu.VMEM((4, 256, SLAB), BF16),
             pltpu.VMEM((4, SLAB, 256), BF16),
             pltpu.VMEM((ROWS, 4, WIDTH, SPAN), BF16),

time: 129 us -> 126 us (0.977)
  Pallas kernels: 122 us -> 119 us
    pallas_call x1, Pallas kernels: 122 us -> 119 us  [body(): pl.pallas_call(kernel, out_shape=(jax.ShapeDtypeStruct(turned.shape, BF16...]
where the time goes in v3:
time: 126 us; the launch traced here: 125 us
  Pallas kernels  119 us (94%)
  local copies, waits for them, and re-layouts  4.41 us (4%)
    pallas_call x1, Pallas kernels, body(): pl.pallas_call(kernel, out_shape=(jax.ShapeDtypeStruct(turned.shape, BF16...  119 us
    unnamed x2, local copies, waits for them, and re-layouts  2.95 us

profile of v3, /device:TPU:32, one launch (start us, length us, event | category | flops | bytes accessed | tf_op | source)
XLA Modules:
  0.0 124.8 jit_solution(15897470174751087618)
XLA Ops:
  0.6 0.8 dynamic_slice.3
  1.4 0.7 stack.10
  2.1 0.6 fusion.6.gains
  2.7 119.2 %shard_map.113 = (bf16[4,288,128]{2,1,0:T(8,128)(2,1)}, bf16[1,4,288]{2,1,0:T(4,128)(2,1)}) custom-call(bf16[4,288,128]{2,1,0:T(8,128)(2,1)} %bitcast.3, bf16[1,4,288]{2,1,0:T(4,128)(2,1)} %critique.1, s32[4]{0:T(128)} %lengths.1, f32[8,384]{1,0:T(8,128)} %fusion.6.gains, f32[2056,128]{1,0:T(8,128)} %constant.15.clone.table_hbm, bf16[4608,256]{1,0:T(8,128)(2,1)} %wq.1, ...), custom_call_target="tpu_custom_call" | custom-call | flops 5000000000 | bytes 16000000 | tf_op jit(solution)/shard_map/pallas_call | solution.py:642
  121.9 1.7 %copy.14 = bf16[4,128,288]{1,2,0:T(8,128)(2,1)} copy(bf16[4,128,288]{1,2,0:T(8,128)(2,1)} %bitcast.2) | data formatting | bytes 589824
  123.6 1.3 %copy.15 = bf16[1,4,288]{2,1,0:T(4,128)(2,1)} copy(bf16[1,4,288]{2,1,0:T(4,128)(2,1)} %get-tuple-element.9) | data formatting | bytes 4608
  (1 shorter events, 0.0 us)

commit v4 on v3

--- a/solution.py
+++ b/solution.py
@@ -17,7 +17,6 @@
 WIDTH = 288
 SLAB = 4 * WIDTH
 HALF = WIDTH // 2
-FIRST = 240
 STEPS = 4
 
 EPS = 1e-06
@@ -27,7 +26,7 @@
 F32 = jnp.float32
 BF16 = jnp.bfloat16
 MESH = pl.DeviceIdType.MESH
-N_SEM = 232
+N_SEM = 184
 
 
 def rope_table():
@@ -129,10 +128,8 @@
 
     zr, zl, zo = (z + 1) % 4, (z + 3) % 4, (z + 2) % 4
     xr, xl, xo = (x + 1) % 4, (x + 3) % 4, (x + 2) % 4
-    main = pl.ds(0, FIRST)
-    main_up, main_down = pl.ds(0, 128), pl.ds(128, FIRST - 128)
-    rest = pl.ds(FIRST, WIDTH - FIRST)
-    rest_up, rest_down = pl.ds(FIRST, 16), pl.ds(FIRST + 16, WIDTH - FIRST - 16)
+    main = pl.ds(0, WIDTH)
+    main_up, main_down = pl.ds(0, HALF), pl.ds(HALF, HALF)
 
     def pair_send(name, up, down, where):
         send(name + (0,), up, up, where(1))
@@ -167,30 +164,9 @@
             recv(("x1", r, k, 1))
         pair_send(("x2", r), xg.at[r, xl, :, main_up], xg.at[r, xr, :, main_down], at_x)
 
-    def b1(r):
-        block = xg.at[r, x, z, rest]
-        pair_send(("b1", r), block, block, at_x)
-
-    def b2(r):
-        recv(("b1", r, 0))
-        recv(("b1", r, 1))
-        pair_send(("b2", r), xg.at[r, xl, z, rest_up], xg.at[r, xr, z, rest_down], at_x)
-
-    def b3(r):
-        recv(("b2", r, 0))
-        recv(("b2", r, 1))
-        block = xg.at[r, :, z, rest]
-        pair_send(("b3", r), block, block, at_z)
-
-    def b4(r):
-        recv(("b3", r, 0))
-        recv(("b3", r, 1))
-        pair_send(("b4", r), xg.at[r, :, zl, rest_up], xg.at[r, :, zr, rest_down], at_z)
-
     def e4(r):
-        for part in ("x2", "b4"):
-            recv((part, r, 0))
-            recv((part, r, 1))
+        recv(("x2", r, 0))
+        recv(("x2", r, 1))
 
     def ow_x():
         for d in (1, 3, 2):
@@ -327,46 +303,41 @@
         return (section * 4 + (y + dy) % 4) * SPAN
 
     def weigh(scores, keep):
-        capped = CAP * jnp.tanh(scores * (SCALE / CAP))
-        return jnp.where(keep, jnp.exp(capped), 0.0)
-
-    def attend(r, j):
-        if j == 0:
-            for dy in range(4):
-                recv(("kvc", r, dy))
-        queries = qbuf[r, j * 128 : j * 128 + 128, :]
+        return jnp.where(keep, jnp.exp2(jnp.tanh(scores * (SCALE / CAP)) * (CAP * math.log2(math.e))), 0.0)
+
+    def attend(r):
+        for dy in range(4):
+            recv(("kvc", r, dy))
+        queries = qbuf[r]
         length = lengths[r]
-        token = (s * 4 + y) * SPAN + lax.broadcasted_iota(jnp.int32, (128, 128), 0)
+        token = (s * 4 + y) * SPAN + lax.broadcasted_iota(jnp.int32, (256, 128), 0) % SPAN
         limit = jnp.minimum(token, length - 1)
-        lane = lax.broadcasted_iota(jnp.int32, (128, 128), 1)
-
-        def step(b, carry):
-            num, den = carry
-            for i in range(4):
-                keys = kvg.at[r, b // 2, (b % 2) * 2 + i // 2, i % 2]
-                weight = weigh(dot(queries, keys[0:128, :]), lane + key_start(b * 4 + i) <= limit)
-                num = num + dot_t(weight.astype(BF16), keys[128:256, :])
-                den = den + weight
-            return num, den
-
-        zero = jnp.zeros((128, 128), F32)
-        num, den = lax.fori_loop(0, 4, step, (zero, zero))
-        attg[r, 0, j] = (num / jnp.sum(den, axis=-1, keepdims=True)).astype(BF16)
-        send(("ax1", r, j, 0), attg.at[r, 0, j], attg.at[r, 3, j], at_x(1))
-        send(("ax1", r, j, 1), attg.at[r, 0, j], attg.at[r, 1, j], at_x(3))
-
-    def ax2(r, j):
-        recv(("ax1", r, j, 0))
-        recv(("ax1", r, j, 1))
-        send(("ax2", r, j, 0), attg.at[r, 3, j, 0:64], attg.at[r, 2, j, 0:64], at_x(1))
-        send(("ax2", r, j, 1), attg.at[r, 1, j, 64:128], attg.at[r, 2, j, 64:128], at_x(3))
+        lane = lax.broadcasted_iota(jnp.int32, (256, 128), 1)
+
+        num = jnp.zeros((256, 128), F32)
+        den = jnp.zeros((256, 128), F32)
+        for i in range(16):
+            keys = kvg.at[r, i // 8, (i // 2) % 4, i % 2]
+            weight = weigh(dot(queries, keys[0:128, :]), lane + key_start(i) <= limit)
+            num = num + dot_t(weight.astype(BF16), keys[128:256, :])
+            den = den + weight
+        result = num / jnp.sum(den, axis=-1, keepdims=True)
+        for k in range(2):
+            attg[r, 0, k] = result[k * 128 : k * 128 + 128].astype(BF16)
+        send(("ax1", r, 0), attg.at[r, 0], attg.at[r, 3], at_x(1))
+        send(("ax1", r, 1), attg.at[r, 0], attg.at[r, 1], at_x(3))
+
+    def ax2(r):
+        recv(("ax1", r, 0))
+        recv(("ax1", r, 1))
+        send(("ax2", r, 0), attg.at[r, 3, 0], attg.at[r, 2, 0], at_x(1))
+        send(("ax2", r, 1), attg.at[r, 1, 1], attg.at[r, 2, 1], at_x(3))
 
     low, high = pl.ds(0, HALF), pl.ds(HALF, HALF)
 
     def proj(r):
-        for j in range(2):
-            recv(("ax2", r, j, 0))
-            recv(("ax2", r, j, 1))
+        recv(("ax2", r, 0))
+        recv(("ax2", r, 1))
         attended = [jnp.concatenate([attg[r, d, 0], attg[r, d, 1]], axis=1) for d in range(4)]
         for dz in (2, 1, 3, 0):
             rows = pl.ds(dz * WIDTH, WIDTH)
@@ -512,117 +483,93 @@
             part = cown[0:4, k * 128 : k * 128 + 128] * factor[8:12, :] * gains[1:2, k * 128 : k * 128 + 128]
             c_out[0, :, lo:hi] = (critique[0, :, lo:hi].astype(F32) + part[:, 0 : hi - lo]).astype(BF16)
 
-    z1(0)
-    c_x()
-    b1(0)
     x1a(0)
-    b1(1)
-    b1(3)
     pre_x()
-    rope_tables()
+    x1a(1)
+    ow_x()
     fetch_weights()
     turn_weights(0, 6)
+    turn_weights(6, 12)
+    rope_tables()
+    c_x()
+    gain_tables()
+    z1(0)
+    turn_weights(12, 18)
+    pre_z()
+    z1(1)
+    e1(0)
+    z1(2)
+    pre_done()
+    ow_y1()
     c_z()
-    b2(0)
-    x1a(1)
-    ow_x()
-    gain_tables()
-    turn_weights(6, 12)
-    turn_weights(12, 18)
-    b2(1)
-    b2(3)
-    e1(0)
-    b3(0)
-    z1(2)
-    pre_z()
-    b1(2)
-    z1(1)
-    ow_y1()
+    e1(1)
+    z1(3)
     e2(0)
     x1a(2)
-    b4(0)
-    b2(2)
+    e1(2)
+    ow_y2()
     e3(0)
-    e1(2)
-    b3(2)
-    pre_done()
+    ow_core()
     c_project()
-    ow_y2()
-    e1(1)
-    b3(1)
-    z1(3)
+    e2(1)
+    x1a(3)
     e4(0)
     project(0)
     kva(0)
+    e1(3)
+    e3(1)
     e2(2)
-    ow_core()
-    b4(2)
+    ow_turn()
     kvc(0)
-    e2(1)
+    kvb(0)
+    e2(3)
+    kvd(0)
+    e4(1)
+    project(1)
+    kve(0)
+    kva(1)
     e3(2)
-    x1a(3)
-    kvb(0)
-    b4(1)
-    e3(1)
-    kvd(0)
-    e1(3)
-    b3(3)
-    kve(0)
+    attend(0)
+    e3(3)
+    kvc(1)
+    kvb(1)
     e4(2)
     project(2)
     kva(2)
-    ow_turn()
-    e2(3)
-    attend(0, 0)
-    e4(1)
-    project(1)
+    ax2(0)
+    kvd(1)
+    kvc(2)
     kvb(2)
-    kvc(2)
-    attend(0, 1)
-    kva(1)
-    b4(3)
-    e3(3)
-    ax2(0, 0)
-    kvd(2)
-    ax2(0, 1)
-    kvb(1)
-    kvc(1)
-    kve(2)
     e4(3)
     project(3)
-    kvd(1)
+    kve(1)
     kva(3)
-    attend(2, 0)
-    attend(2, 1)
-    kve(1)
     proj(0)
-    ax2(2, 0)
+    kvd(2)
+    attend(1)
+    kvc(3)
     kvb(3)
-    kvc(3)
-    attend(1, 0)
-    ax2(2, 1)
-    attend(1, 1)
+    kve(2)
     rs_2(0)
+    ax2(1)
+    attend(2)
     kvd(3)
-    ax2(1, 0)
-    proj(2)
-    ax2(1, 1)
-    kve(3)
     rs_3(0)
     proj(1)
-    attend(3, 0)
+    kve(3)
+    ax2(2)
+    attend(3)
+    rs_2(1)
+    c_attend()
+    proj(2)
+    ax2(3)
+    c_proj()
+    rs_3(1)
+    proj(3)
     rs_2(2)
-    attend(3, 1)
-    c_attend()
-    ax2(3, 0)
-    rs_2(1)
-    ax2(3, 1)
-    c_proj()
-    proj(3)
-    rs_3(2)
-    rs_3(1)
     c_sum()
     rs_2(3)
+    rs_3(2)
     rs_3(3)
     sum_x()
     sum_z()

time: 126 us -> 116 us (0.921)
  Pallas kernels: 119 us -> 110 us
    pallas_call x1, Pallas kernels: 119 us -> 110 us  [body(): pl.pallas_call(kernel, out_shape=(jax.ShapeDtypeStruct(turned.shape, BF16...]
where the time goes in v4:
time: 116 us
  Pallas kernels  110 us (95%)
  local copies, waits for them, and re-layouts  4.41 us (4%)
    pallas_call x1, Pallas kernels, body(): pl.pallas_call(kernel, out_shape=(jax.ShapeDtypeStruct(turned.shape, BF16...  110 us
    unnamed x2, local copies, waits for them, and re-layouts  2.95 us

profile of v4, /device:TPU:32, one launch (start us, length us, event | category | flops | bytes accessed | tf_op | source)
XLA Modules:
  0.0 116.0 jit_solution(14299073762197615901)
XLA Ops:
  0.6 0.8 dynamic_slice.3
  1.4 0.7 stack.10
  2.1 0.6 fusion.6.gains
  2.7 110.4 %shard_map.113 = (bf16[4,288,128]{2,1,0:T(8,128)(2,1)}, bf16[1,4,288]{2,1,0:T(4,128)(2,1)}) custom-call(bf16[4,288,128]{2,1,0:T(8,128)(2,1)} %bitcast.3, bf16[1,4,288]{2,1,0:T(4,128)(2,1)} %critique.1, s32[4]{0:T(128)} %lengths.1, f32[8,384]{1,0:T(8,128)} %fusion.6.gains, f32[2056,128]{1,0:T(8,128)} %constant.15.clone.table_hbm, bf16[4608,256]{1,0:T(8,128)(2,1)} %wq.1, ...), custom_call_target="tpu_custom_call" | custom-call | flops 5000000000 | bytes 16000000 | tf_op jit(solution)/shard_map/pallas_call | solution.py:589
  113.1 1.7 %copy.14 = bf16[4,128,288]{1,2,0:T(8,128)(2,1)} copy(bf16[4,128,288]{1,2,0:T(8,128)(2,1)} %bitcast.2) | data formatting | bytes 589824
  114.8 1.3 %copy.15 = bf16[1,4,288]{2,1,0:T(4,128)(2,1)} copy(bf16[1,4,288]{2,1,0:T(4,128)(2,1)} %get-tuple-element.9) | data formatting | bytes 4608
  (1 shorter events, 0.0 us)

commit v5 on v4

--- a/solution.py
+++ b/solution.py
@@ -483,46 +483,46 @@
             part = cown[0:4, k * 128 : k * 128 + 128] * factor[8:12, :] * gains[1:2, k * 128 : k * 128 + 128]
             c_out[0, :, lo:hi] = (critique[0, :, lo:hi].astype(F32) + part[:, 0 : hi - lo]).astype(BF16)
 
+    x1a(1)
+    z1(0)
     x1a(0)
-    pre_x()
-    x1a(1)
+    c_x()
     ow_x()
     fetch_weights()
     turn_weights(0, 6)
+    pre_x()
     turn_weights(6, 12)
+    turn_weights(12, 18)
+    z1(1)
     rope_tables()
-    c_x()
     gain_tables()
-    z1(0)
-    turn_weights(12, 18)
-    pre_z()
-    z1(1)
     e1(0)
+    c_z()
     z1(2)
-    pre_done()
-    ow_y1()
-    c_z()
     e1(1)
     z1(3)
     e2(0)
+    ow_y1()
     x1a(2)
-    e1(2)
+    pre_z()
     ow_y2()
     e3(0)
-    ow_core()
-    c_project()
+    e1(2)
     e2(1)
     x1a(3)
+    ow_core()
     e4(0)
+    e1(3)
+    pre_done()
     project(0)
+    c_project()
     kva(0)
-    e1(3)
     e3(1)
     e2(2)
+    e2(3)
     ow_turn()
     kvc(0)
     kvb(0)
-    e2(3)
     kvd(0)
     e4(1)
     project(1)
@@ -530,8 +530,8 @@
     kva(1)
     e3(2)
     attend(0)
+    kvc(1)
     e3(3)
-    kvc(1)
     kvb(1)
     e4(2)
     project(2)
@@ -542,8 +542,8 @@
     kvb(2)
     e4(3)
     project(3)
+    kva(3)
     kve(1)
-    kva(3)
     proj(0)
     kvd(2)
     attend(1)
@@ -576,6 +576,11 @@
     finish()
     for copy in copies.values():
         copy.wait_send()
+
+
+def hand_over(result, c_result, out, c_out):
+    out[...] = result[...]
+    c_out[...] = c_result[...]
 
 
 def body(hidden, critique, lengths, pre_gain, post_gain, q_weight, k_weight, v_weight, o_weight):
@@ -632,6 +637,15 @@
         ),
         cost_estimate=pl.CostEstimate(flops=5_000_000_000, bytes_accessed=16_000_000, transcendentals=4_000_000),
     )(turned, critique, lengths, gains, table, q_weight, k_weight, v_weight, o_weight)
+    result, c_result = pl.pallas_call(
+        hand_over,
+        out_shape=(
+            jax.ShapeDtypeStruct(turned.shape, BF16),
+            jax.ShapeDtypeStruct(critique.shape, BF16),
+        ),
+        in_specs=[vmem, vmem],
+        out_specs=(vmem, vmem),
+    )(result, c_result)
     return jnp.transpose(result, (0, 2, 1)), c_result
 
 

time: 116 us -> 113 us (0.974)
  local copies, waits for them, and re-layouts: 4.41 us -> 1.46 us
    unnamed x2 -> x0, local copies, waits for them, and re-layouts: 2.95 us -> none
    pallas_call x0 -> x1, Pallas kernels: none -> 1.7 us  [body(): pl.pallas_call(hand_over, out_shape=(jax.ShapeDtypeStruct(turned.shape, B...]
    pallas_call x1, Pallas kernels: 110 us -> 109 us  [body(): pl.pallas_call(kernel, out_shape=(jax.ShapeDtypeStruct(turned.shape, BF16...]
where the time goes in v5:
time: 113 us
  Pallas kernels  110 us (97%)
  local copies, waits for them, and re-layouts  1.46 us (1%)
    pallas_call x1, Pallas kernels, body(): pl.pallas_call(kernel, out_shape=(jax.ShapeDtypeStruct(turned.shape, BF16...  109 us

profile of v5, /device:TPU:32, one launch (start us, length us, event | category | flops | bytes accessed | tf_op | source)
XLA Modules:
  0.0 113.2 jit_solution(9143467995598508608)
XLA Ops:
  0.6 0.8 dynamic_slice.3
  1.4 0.7 stack.10
  2.1 0.6 fusion.6.gains
  2.7 108.7 %shard_map.113 = (bf16[4,288,128]{2,1,0:T(8,128)(2,1)}, bf16[1,4,288]{2,1,0:T(4,128)(2,1)}) custom-call(bf16[4,288,128]{2,1,0:T(8,128)(2,1)} %bitcast.2, bf16[1,4,288]{2,1,0:T(4,128)(2,1)} %critique.1, s32[4]{0:T(128)} %lengths.1, f32[8,384]{1,0:T(8,128)} %fusion.6.gains, f32[2056,128]{1,0:T(8,128)} %constant.15.clone.table_hbm, bf16[4608,256]{1,0:T(8,128)(2,1)} %wq.1, ...), custom_call_target="tpu_custom_call" | custom-call | flops 5000000000 | bytes 16000000 | tf_op jit(solution)/shard_map/pallas_call | solution.py:594
  111.5 1.7 %shard_map.114 = (bf16[4,288,128]{2,1,0:T(8,128)(2,1)}, bf16[1,4,288]{2,1,0:T(4,128)(2,1)}) custom-call(bf16[4,288,128]{2,1,0:T(8,128)(2,1)} %get-tuple-element.6.result, bf16[1,4,288]{2,1,0:T(4,128)(2,1)} %get-tuple-element.7.c_result), custom_call_target="tpu_custom_call" | custom-call | tf_op jit(solution)/shard_map/pallas_call | solution.py:640
  (1 shorter events, 0.0 us)

commit v6 on v5

--- a/solution.py
+++ b/solution.py
@@ -44,10 +44,10 @@
 
 
 def kernel(
-    hidden, critique, lengths, gains, table_hbm, wq, wk, wv, wo,
+    hidden, critique, lengths, pre_gain, post_gain, table_hbm, wq, wk, wv, wo,
     out, c_out,
     xg, wraw, wt, pgb, table, cosT, sinT, qbuf, kvg, attg, owslab, owt,
-    pb, own, rs1, rs2, cg, cq, ckv, cattg, cpj, cown, crs, ssx, ssz, prex, prez, fac,
+    pb, own, rs1, rs2, cg, cq, ckv, cattg, cpj, cown, crs, ssx, ssz, prex, prez, fac, gains,
     send_sem, recv_sem, local_sem,
 ):
     s = lax.axis_index("section")
@@ -105,6 +105,12 @@
     ]
     fetch_table = fetch(table_hbm, table)
     fetch_o = fetch(wo.at[pl.ds(piece, 32), own_cols], owslab.at[0, pl.ds(piece, 32), :])
+
+    mine = lax.broadcasted_iota(jnp.int32, (16, WIDTH), 0) == h
+    own_gain = jnp.sum(jnp.where(mine, pre_gain[...].astype(F32), 0.0), axis=0, keepdims=True)
+    gains[...] = jnp.zeros((8, 384), F32)
+    gains[0:1, 0:WIDTH] = own_gain
+    gains[1:2, 0:WIDTH] = post_gain[...].astype(F32)
 
     def column(row, k):
         n = 128 if k < 2 else 32
@@ -584,8 +590,6 @@
 
 
 def body(hidden, critique, lengths, pre_gain, post_gain, q_weight, k_weight, v_weight, o_weight):
-    own_gain = lax.dynamic_slice(pre_gain, (lax.axis_index("head") * WIDTH,), (WIDTH,))
-    gains = jnp.pad(jnp.stack([own_gain, post_gain]).astype(F32), ((0, 6), (0, 384 - WIDTH)))
     table = jnp.asarray(rope_table())
     vmem = pl.BlockSpec(memory_space=pltpu.VMEM)
     smem = pl.BlockSpec(memory_space=pltpu.SMEM)
@@ -597,7 +601,7 @@
             jax.ShapeDtypeStruct(turned.shape, BF16),
             jax.ShapeDtypeStruct(critique.shape, BF16),
         ),
-        in_specs=[vmem, vmem, smem, vmem, anywhere, anywhere, anywhere, anywhere, anywhere],
+        in_specs=[vmem, vmem, smem, vmem, vmem, anywhere, anywhere, anywhere, anywhere, anywhere],
         out_specs=(vmem, vmem),
         scratch_shapes=[
             pltpu.VMEM((ROWS, 4, 4, WIDTH, SPAN), BF16),
@@ -628,6 +632,7 @@
             pltpu.VMEM((4, 16, 128), F32),
             pltpu.VMEM((4, 16, 128), F32),
             pltpu.VMEM((16, 128), F32),
+            pltpu.VMEM((8, 384), F32),
             pltpu.SemaphoreType.DMA((N_SEM,)),
             pltpu.SemaphoreType.DMA((N_SEM,)),
             pltpu.SemaphoreType.DMA((8,)),
@@ -636,7 +641,7 @@
             collective_id=0, has_side_effects=True, vmem_limit_bytes=56 * 1024 * 1024
         ),
         cost_estimate=pl.CostEstimate(flops=5_000_000_000, bytes_accessed=16_000_000, transcendentals=4_000_000),
-    )(turned, critique, lengths, gains, table, q_weight, k_weight, v_weight, o_weight)
+    )(turned, critique, lengths, pre_gain.reshape(16, WIDTH), post_gain.reshape(1, WIDTH), table, q_weight, k_weight, v_weight, o_weight)
     result, c_result = pl.pallas_call(
         hand_over,
         out_shape=(

time: 113 us -> 114 us (level)
  local copies, waits for them, and re-layouts: 1.46 us -> 2.63 us
    reshape x0 -> x2, local copies, waits for them, and re-layouts: none -> 2.63 us  [the longest x1 1.39 us: body(): pre_gain.reshape(16, WIDTH)]
where the time goes in v6:
time: 114 us
  Pallas kernels  111 us (97%)
  local copies, waits for them, and re-layouts  2.63 us (2%)
    pallas_call x1, Pallas kernels, body(): pl.pallas_call(kernel, out_shape=(jax.ShapeDtypeStruct(turned.shape, BF16...  109 us

profile of v6, /device:TPU:32, one launch (start us, length us, event | category | flops | bytes accessed | tf_op | source)
XLA Modules:
  0.0 113.8 jit_solution(12603146653268390340)
XLA Ops:
  0.6 1.2 %reshape.11.post_gain = bf16[1,288]{1,0:T(2,128)(2,1)} reshape(bf16[288]{0:T(512)(128)(2,1)} %param.14) | data formatting | bytes 1152 | tf_op jit(solution)/shard_map/reshape | solution.py:644
  1.9 1.4 %reshape.10.pre_gain = bf16[16,288]{1,0:T(8,128)(2,1)} reshape(bf16[4608]{0:T(1024)(128)(2,1)} %param.13) | data formatting | bytes 18432 | tf_op jit(solution)/shard_map/reshape | solution.py:644
  3.3 108.9 %shard_map.113 = (bf16[4,288,128]{2,1,0:T(8,128)(2,1)}, bf16[1,4,288]{2,1,0:T(4,128)(2,1)}) custom-call(bf16[4,288,128]{2,1,0:T(8,128)(2,1)} %bitcast.2, bf16[1,4,288]{2,1,0:T(4,128)(2,1)} %critique.1, s32[4]{0:T(128)} %lengths.1, bf16[16,288]{1,0:T(8,128)(2,1)} %reshape.10.pre_gain, bf16[1,288]{1,0:T(2,128)(2,1)} %reshape.11.post_gain, ...), custom_call_target="tpu_custom_call" | custom-call | flops 5000000000 | bytes 16000000 | tf_op jit(solution)/shard_map/pallas_call | solution.py:598
  112.1 1.7 %shard_map.114 = (bf16[4,288,128]{2,1,0:T(8,128)(2,1)}, bf16[1,4,288]{2,1,0:T(4,128)(2,1)}) custom-call(bf16[4,288,128]{2,1,0:T(8,128)(2,1)} %get-tuple-element.6.result, bf16[1,4,288]{2,1,0:T(4,128)(2,1)} %get-tuple-element.7.c_result), custom_call_target="tpu_custom_call" | custom-call | tf_op jit(solution)/shard_map/pallas_call | solution.py:645

commit v7 on v5

--- a/solution.py
+++ b/solution.py
@@ -484,92 +484,92 @@
             c_out[0, :, lo:hi] = (critique[0, :, lo:hi].astype(F32) + part[:, 0 : hi - lo]).astype(BF16)
 
     x1a(1)
-    z1(0)
+    fetch_weights()
     x1a(0)
-    c_x()
-    ow_x()
-    fetch_weights()
     turn_weights(0, 6)
     pre_x()
     turn_weights(6, 12)
     turn_weights(12, 18)
+    ow_x()
+    gain_tables()
+    z1(0)
+    c_x()
+    rope_tables()
     z1(1)
-    rope_tables()
-    gain_tables()
+    pre_z()
     e1(0)
+    z1(2)
+    ow_y1()
     c_z()
-    z1(2)
     e1(1)
     z1(3)
+    pre_done()
     e2(0)
-    ow_y1()
     x1a(2)
-    pre_z()
+    e1(2)
     ow_y2()
     e3(0)
-    e1(2)
+    ow_core()
+    c_project()
     e2(1)
     x1a(3)
-    ow_core()
     e4(0)
-    e1(3)
-    pre_done()
     project(0)
-    c_project()
     kva(0)
     e3(1)
+    e1(3)
     e2(2)
+    ow_turn()
+    kvb(0)
+    kvc(0)
     e2(3)
-    ow_turn()
-    kvc(0)
-    kvb(0)
-    kvd(0)
     e4(1)
     project(1)
+    kvd(0)
+    kva(1)
     kve(0)
-    kva(1)
+    kvb(1)
     e3(2)
+    kvc(1)
     attend(0)
-    kvc(1)
     e3(3)
-    kvb(1)
+    kvd(1)
     e4(2)
     project(2)
+    kve(1)
     kva(2)
     ax2(0)
-    kvd(1)
+    attend(1)
     kvc(2)
     kvb(2)
     e4(3)
     project(3)
     kva(3)
-    kve(1)
     proj(0)
+    ax2(1)
     kvd(2)
-    attend(1)
+    proj(1)
+    kve(2)
+    kvb(3)
+    rs_2(0)
     kvc(3)
-    kvb(3)
-    kve(2)
-    rs_2(0)
-    ax2(1)
     attend(2)
     kvd(3)
-    rs_3(0)
-    proj(1)
+    rs_2(1)
     kve(3)
     ax2(2)
+    rs_3(0)
     attend(3)
-    rs_2(1)
+    proj(2)
+    rs_3(1)
     c_attend()
-    proj(2)
     ax2(3)
     c_proj()
-    rs_3(1)
+    rs_2(2)
     proj(3)
-    rs_2(2)
     c_sum()
+    rs_3(2)
     rs_2(3)
-    rs_3(2)
     rs_3(3)
     sum_x()
     sum_z()

time: 113 us -> 120 us (1.062)
  Pallas kernels: 110 us -> 117 us
    pallas_call x1, Pallas kernels: 109 us -> 116 us  [body(): pl.pallas_call(kernel, out_shape=(jax.ShapeDtypeStruct(turned.shape, BF16...]
where the time goes in v7:
time: 120 us
  Pallas kernels  117 us (98%)
  local copies, waits for them, and re-layouts  1.46 us (1%)
    pallas_call x1, Pallas kernels, body(): pl.pallas_call(kernel, out_shape=(jax.ShapeDtypeStruct(turned.shape, BF16...  116 us

profile of v7, /device:TPU:32, one launch (start us, length us, event | category | flops | bytes accessed | tf_op | source)
XLA Modules:
  0.0 119.9 jit_solution(1158870699838022078)
XLA Ops:
  0.6 0.8 dynamic_slice.3
  1.4 0.7 stack.10
  2.1 0.6 fusion.6.gains
  2.7 115.5 %shard_map.113 = (bf16[4,288,128]{2,1,0:T(8,128)(2,1)}, bf16[1,4,288]{2,1,0:T(4,128)(2,1)}) custom-call(bf16[4,288,128]{2,1,0:T(8,128)(2,1)} %bitcast.2, bf16[1,4,288]{2,1,0:T(4,128)(2,1)} %critique.1, s32[4]{0:T(128)} %lengths.1, f32[8,384]{1,0:T(8,128)} %fusion.6.gains, f32[2056,128]{1,0:T(8,128)} %constant.15.clone.table_hbm, bf16[4608,256]{1,0:T(8,128)(2,1)} %wq.1, ...), custom_call_target="tpu_custom_call" | custom-call | flops 5000000000 | bytes 16000000 | tf_op jit(solution)/shard_map/pallas_call | solution.py:594
  118.2 1.7 %shard_map.114 = (bf16[4,288,128]{2,1,0:T(8,128)(2,1)}, bf16[1,4,288]{2,1,0:T(4,128)(2,1)}) custom-call(bf16[4,288,128]{2,1,0:T(8,128)(2,1)} %get-tuple-element.6.result, bf16[1,4,288]{2,1,0:T(4,128)(2,1)} %get-tuple-element.7.c_result), custom_call_target="tpu_custom_call" | custom-call | tf_op jit(solution)/shard_map/pallas_call | solution.py:640
  (1 shorter events, 0.0 us)
